TPU v7x, 256 devices: a whole 4x4x8 slice. The times are simulated.
256 devices in a mesh: row: 16 (over x, y), col: 16 (over z, core).
Axes of the slice: x: 4, y: 4, z: 8, core: 2. Of those that a mesh axis runs over, the one named last changes fastest.
Arguments:
- diag_tiles: float32 [1, 16, 1024, 1024], P(None, 'row', 'col')
- left_factors: bfloat16 [1, 16, 1, 16, 1024, 256], P(None, 'row', None, 'col'), as said below
- right_factors: bfloat16 [1, 16, 1, 16, 1024, 256], P(None, 'row', None, 'col'), as said below
- ranks: int32 [1, 16, 1, 16], P(None, 'row', None, 'col'), may hold values from 32 to 256, as said below
Outputs:
- new_diag: float32 [1, 16, 1024, 1024], P(None, 'row', 'col')
- updates: bfloat16 [1, 16, 1, 16, 1024, 768], P(None, 'row', None, 'col')
Inputs may be any that keep to these rules, and one draw needn't show every extreme that they name: `ranks`: every tile (i, i - 1) has rank 256. `left_factors`: columns at or beyond a tile's rank hold values that are not read. `right_factors`: columns at or beyond a tile's rank hold values that are not read.
All inputs are finite; a program needn't handle non-finite values.
Results may differ from a plain program's by a relative error of at most 0.014.
Values may be sent and summed in bfloat16 or wider, within the bound.
No kernel may reach another device: no remote copies, remote signals or barrier semaphores. Data moves between devices by JAX's collectives and lax.ppermute only.
A program may use at most 128 MiB of HBM per device.

v0:
```python
import functools

import jax
import jax.numpy as jnp
from jax import lax
from jax.experimental import pallas as pl
from jax.experimental.pallas import tpu as pltpu
from jax.sharding import PartitionSpec as P

F32 = jnp.float32
BF16 = jnp.bfloat16
NB = 1024
RANK = 256
BLK = 128
NBLK = NB // BLK
BAND = 5 * BLK
SPAN = 4
TILE1 = 2 * BAND + 2 * RANK
TN = (((0,), (0,)), ((), ()))
NT = (((1,), (1,)), ((), ()))
VMEM = pl.BlockSpec(memory_space=pltpu.VMEM)
SMEM = pl.BlockSpec(memory_space=pltpu.SMEM)
ANY = pl.BlockSpec(memory_space=pl.ANY)


def grant(mib):
    return pltpu.CompilerParams(vmem_limit_bytes=mib * 1024 * 1024)


def lanes_of(x, c):
    return jnp.broadcast_to(x[:, c : c + 1], (8, BLK))


def rows_of(x, r):
    return jnp.broadcast_to(x[r : r + 1, :], (8, BLK))


def factor_block(rows):
    sub = lax.broadcasted_iota(jnp.int32, (8, BLK), 0)
    lane = lax.broadcasted_iota(jnp.int32, (8, BLK), 1)
    a = list(rows)
    n = len(a)
    up, inv, wide = [], [], []
    cols = [lanes_of(a[0], m) for m in range(8)]
    for g in range(n):
        c0 = 8 * g
        near = min(n, g // SPAN * SPAN + 2 * SPAN)
        here = (lane >= c0) & (lane < c0 + 8)
        left = [[lanes_of(a[b], c0 + m) for m in range(8)] for b in range(g + 1, near)]
        ahead = [lanes_of(a[g + 1], c0 + 8 + m) for m in range(8)] if g + 1 < n else None
        mult, recip, piv = [], [], None
        for k in range(8):
            d = rows_of(cols[k], k)
            r = 1.0 / d
            recip.append(r)
            piv = d if piv is None else jnp.where(sub == k, d, piv)
            for m in range(k + 1, 8):
                cols[m] = cols[m] - (cols[k] * rows_of(cols[k], m)) * r
            mult.append(jnp.where(sub > k, cols[k] * r, 0.0))
        s = jnp.where(here, jnp.where(lane == c0 + sub, 1.0, 0.0), a[g])
        s2 = a[g]
        for k in range(7):
            s = s - mult[k] * rows_of(s, k)
            s2 = s2 - mult[k] * rows_of(s2, k)
        root = lax.rsqrt(piv)
        r_ = s * root
        t = r_ * root
        diag = jnp.where(lane >= c0 + sub, s2 * root, 0.0)
        up.append(jnp.where(here, diag, jnp.where(lane >= c0 + 8, r_, 0.0)))
        inv.append(jnp.where(lane < c0 + 8, r_, 0.0))
        if g + 1 == n:
            break
        mk = [[rows_of(mult[k], m) if m > k else None for m in range(8)] for k in range(8)]
        tk = [rows_of(t, k) for k in range(8)]
        for b in range(g + 1, near):
            x = left[b - g - 1]
            for k in range(8):
                for m in range(k + 1, 8):
                    x[m] = x[m] - x[k] * mk[k][m]
            if b == g + 1:
                cols = ahead
                for k in range(8):
                    xs = x[k] * recip[k]
                    for m in range(8):
                        cols[m] = cols[m] - x[k] * rows_of(xs, m)
            new = jnp.where(here, 0.0, a[b])
            for k in range(8):
                new = new - x[k] * tk[k]
            a[b] = new
        wide.append(jnp.where((lane >= c0 + 8) & (lane < 8 * (g // SPAN * SPAN + SPAN)), 0.0, r_))
        if (g + 1) % SPAN == 0 and near < n:
            hi, lo = split(jnp.concatenate(wide, axis=0))
            wide = []
            both = tn32(hi, hi) + (tn32(hi, lo) + tn32(lo, hi))
            done = (lane >= c0 + 8 - 8 * SPAN) & (lane < c0 + 8)
            for b in range(near, n):
                a[b] = jnp.where(done, 0.0, a[b]) - both[8 * b : 8 * b + 8]
    return up, inv


def split(x):
    hi = x.astype(BF16)
    return hi, (x - hi.astype(F32)).astype(BF16)


def tn32(a, b):
    return lax.dot_general(a, b, TN, preferred_element_type=F32)


def tn(a, b):
    return tn32(a, b).astype(BF16)


def mm(a, b):
    return jnp.dot(a, b, preferred_element_type=F32)


def mm3(a, b):
    return mm(a[0], b[0]) + (mm(a[0], b[1]) + mm(a[1], b[0]))


def unfold(work, take):
    for r in range(NBLK):
        n = min(5, NBLK - r)
        rows = slice(r * BLK, (r + 1) * BLK)
        work[rows, r * BLK : (r + n) * BLK] = take(r, slice(0, n * BLK))
        for c in range(r + 5, NBLK):
            o = (NBLK - (c - r)) * BLK
            work[rows, c * BLK : (c + 1) * BLK] = take(c, slice(o, o + BLK)).T


def cholesky_blocks(work, lb, mh, ml, inv_s):
    def body(k, _):
        off = pl.multiple_of(k * BLK, BLK)
        rows = [work[pl.ds(pl.multiple_of(off + 8 * i, 8), 8), pl.ds(off, BLK)] for i in range(16)]
        up, inv = factor_block(rows)
        for i in range(16):
            inv_s[8 * i : 8 * i + 8, :] = inv[i]
        work[pl.ds(off, BLK), pl.ds(off, BLK)] = jnp.concatenate(up, axis=0).T
        hi, lo = split(inv_s[...])
        mh[pl.ds(off, BLK), :] = hi
        ml[pl.ds(off, BLK), :] = lo
        for kk in range(NBLK - 1):

            @pl.when(k == kk)
            def _():
                o = BLK * kk
                e = o + BLK
                upper = mm3((hi, lo), split(work[o:e, e:]))
                parts = split(upper)
                for ib in range(kk + 1, NBLK):
                    i0 = BLK * ib
                    c = i0 - e
                    low = upper[:, c : c + BLK].T
                    lows = split(low)
                    lb[i0 : i0 + BLK, o:e] = lows[0]
                    work[i0 : i0 + BLK, o:e] = low
                    work[i0 : i0 + BLK, i0:] = work[i0 : i0 + BLK, i0:] - mm3(
                        lows, (parts[0][:, c:], parts[1][:, c:])
                    )

        return 0

    lax.fori_loop(0, NBLK, body, 0)


def write_rows(place, work, lrow):
    start = pl.multiple_of(64 * (2 * place[0] + place[1]), 64)
    r = lax.broadcasted_iota(jnp.int32, (64, NB), 0) + start
    c = lax.broadcasted_iota(jnp.int32, (64, NB), 1)
    lrow[...] = jnp.where(c <= r, work[pl.ds(start, 64), :], 0.0)


def fetch(pairs, sems):
    copies = [pltpu.make_async_copy(src, dst, sems.at[n]) for n, (src, dst) in enumerate(pairs)]
    for one in copies:
        one.start()
    return copies


def first_kernel(place, raw_h, lrow, lb, mh, ml, raw, work, inv_s, sems):
    for one in fetch([(raw_h, raw)], sems):
        one.wait()
    unfold(work, lambda r, cols: raw[r * BLK : (r + 1) * BLK, cols])
    cholesky_blocks(work, lb, mh, ml, inv_s)
    write_rows(place, work, lrow)


def solve_step(k, w, lb, mh, ml, p):
    o = BLK * k
    e = o + BLK
    x = mm3((mh[o:e, :], ml[o:e, :]), split(w[o:e, :]))
    p[o:e, :] = x.astype(BF16)
    if e < NB:
        xs = split(x)
        low = lb[e:, o:e]
        w[e:, :] = w[e:, :] - (mm(low, xs[0]) + mm(low, xs[1]))


def second_kernel(
    place, tile_h, lb0_h, mh0_h, ml0_h, lrow, lb, mh, ml, p10, tile, lb0, mh0, ml0, work, w, inv_s, sems
):
    copies = fetch([(tile_h.at[:, : TILE1 + 2 * RANK], tile), (mh0_h, mh0), (ml0_h, ml0), (lb0_h, lb0)], sems)
    for one in copies:
        one.wait()
    w[:, :RANK] = tile[:, 2 * BAND + RANK : TILE1].astype(F32)
    w[:, RANK:] = tile[:, TILE1 + RANK : TILE1 + 2 * RANK].astype(F32)
    for k in range(NBLK):
        solve_step(k, w, lb0, mh0, ml0, p10)
    solved = p10[:, :RANK]
    inner = lax.dot_general(solved, solved, TN, preferred_element_type=F32).astype(BF16)
    u = tile[:, 2 * BAND : 2 * BAND + RANK]
    corr = split(mm(u, inner))

    def take(r, cols):
        rows = slice(r * BLK, (r + 1) * BLK)
        return tile[rows, cols].astype(F32) + tile[rows, cols.start + BAND : cols.stop + BAND].astype(F32)

    unfold(work, take)
    for r in range(NBLK):
        o = r * BLK
        right = u[o:, :]
        work[o : o + BLK, o:] = work[o : o + BLK, o:] - (
            lax.dot_general(corr[0][o : o + BLK], right, NT, preferred_element_type=F32)
            + lax.dot_general(corr[1][o : o + BLK], right, NT, preferred_element_type=F32)
        )
    cholesky_blocks(work, lb, mh, ml, inv_s)
    write_rows(place, work, lrow)


def last_kernel(place, *refs):
    parts, (tile_h, p10i_h, diag_h, lrow0_h, lrow1_h) = refs[:4], refs[4:9]
    lb0_h, mh0_h, ml0_h, lb1_h, mh1_h, ml1_h, new, upd = refs[9:17]
    (cols, rows, u10, p10i, diag, lrow0, lrow1, lb0, mh0, ml0, lb1, mh1, ml1, w0, w1, pj, p1, sems) = refs[17:]
    j = 2 * place[0] + place[1]
    i = place[2]
    x, y = i // 4, lax.rem(i, 4)
    pairs = [(tile_h.at[:, TILE1:], rows), (tile_h.at[:, 2 * BAND : 2 * BAND + RANK], u10)]
    for b in range(4):
        for a in range(4):
            k = 4 * lax.rem(x + 4 - a, 4) + lax.rem(y + 4 - b, 4)
            pairs.append((parts[b].at[pl.ds(64 * a, 64)], cols.at[pl.ds(pl.multiple_of(64 * k, 64), 64)]))
    head = len(pairs)
    pairs += [(mh0_h, mh0), (ml0_h, ml0), (mh1_h, mh1), (ml1_h, ml1), (lb0_h, lb0), (lb1_h, lb1)]
    body = len(pairs)
    pairs += [(p10i_h, p10i), (diag_h, diag), (lrow0_h, lrow0), (lrow1_h, lrow1)]
    copies = fetch(pairs, sems)
    for one in copies[:head]:
        one.wait()
    w0[...] = cols[:, :RANK].astype(F32)
    w1[:, :RANK] = rows[:, 3 * RANK :].astype(F32)
    w1[:, RANK : 2 * RANK] = u10[...].astype(F32)
    w1[:, 2 * RANK :] = cols[:, RANK:].astype(F32)
    for one in copies[head:body]:
        one.wait()
    for k in range(NBLK):
        solve_step(k, w0, lb0, mh0, ml0, pj)
        solve_step(k, w1, lb1, mh1, ml1, p1)
    for one in copies[body:]:
        one.wait()
    zero = jnp.zeros((), BF16)
    pi = jnp.where(i > 0, p10i[:, RANK:], zero)
    ui = rows[:, :RANK]
    start = pl.multiple_of(64 * j, 64)
    ui_part = rows[pl.ds(start, 64), :RANK]
    inner01 = tn(pi, p10i[:, :RANK])
    c0 = mm(ui, tn(pi, pj[...])).astype(BF16)
    c01 = mm(ui, inner01).astype(BF16)
    c0_part = mm(ui_part, tn(pi, pi)).astype(BF16)
    d = diag[...] - lax.dot_general(c0_part, ui, NT, preferred_element_type=F32)
    upd[:, :RANK] = jnp.where(j == 0, pi, jnp.where((i > j) & (j > 0), c0, zero))
    q = jnp.where(i > 1, p1[...], zero)
    q_i = q[:, : 2 * RANK]
    square = tn(q_i, q_i)
    inner = jnp.concatenate([tn(q_i, q[:, 2 * RANK :]), square[:, RANK:]], axis=1)
    up = jnp.concatenate([rows[:, 2 * RANK : 3 * RANK], -c01], axis=1)
    c1 = mm(up, inner).astype(BF16)
    up_part = jnp.concatenate(
        [rows[pl.ds(start, 64), 2 * RANK : 3 * RANK], -mm(ui_part, inner01).astype(BF16)], axis=1
    )
    c1_part = mm(up_part, square).astype(BF16)
    d = d - lax.dot_general(c1_part, up, NT, preferred_element_type=F32)
    new[...] = jnp.where(i == 0, lrow0[...], jnp.where(i == 1, lrow1[...], d))
    upd[:, RANK:] = jnp.where(j == 1, q_i, jnp.where((i > j) & (j > 1), c1, zero))


def shape(rows, cols, dtype):
    return jax.ShapeDtypeStruct((rows, cols), dtype)


FACTOR = [shape(64, NB, F32), shape(NB, NB, BF16), shape(NB, BLK, BF16), shape(NB, BLK, BF16)]


def swap_core(x):
    return lax.ppermute(x, "col", [(c, c ^ 1) for c in range(16)])


def after(x, *tokens):
    return lax.optimization_barrier((x, *tokens))[0]


def at(row, col):
    return 16 * row + col


def pick(cases, default):
    for hit, x in cases:
        default = jnp.where(hit, x, default)
    return default


def spread_x(x, row_at, rows):
    got = [lax.ppermute(x, "row", [(y, 4 * k + y) for y in rows]) for k in (1, 2, 3)]
    return pick([(row_at // 4 == k, got[k - 1]) for k in (1, 2, 3)], x)


def spread_y(x, row_at, rows):
    got = [lax.ppermute(x, "row", [(4 * a + y, 4 * a + (y + s) % 4) for a in range(4) for y in rows]) for s in (1, 2, 3)]
    return [pick([(row_at % 4 == (y + s) % 4, got[s - 1]) for s in (1, 2, 3)], x) for y in rows]


def halve(x, z, gap):
    half = x.shape[0] // 2
    pairs = [(2 * a + c, 2 * (a + gap) + c) for a in range(0, 8, 2 * gap) for c in (0, 1)]
    got = lax.ppermute(x[half:], "col", pairs)
    return jnp.where((z // gap) % 2 == 1, got, x[:half])


def deal(cur, z, core, tokens):
    first = core == 0

    def chunk(q0, q1):
        return jnp.where(first, cur[64 * q0 : 64 * q0 + 64], cur[64 * q1 : 64 * q1 + 64])

    def send(x, step, flip):
        pairs = [(2 * a + c, 2 * (a + step) + (c ^ flip)) for a in range(0, 8, 2) for c in (0, 1)]
        return lax.ppermute(after(x, *tokens), "col", pairs)

    odd = z % 2 == 1
    same = jnp.where(odd, send(chunk(2, 3), 1, 0), chunk(0, 1))
    cross = jnp.where(odd, send(chunk(3, 2), 1, 1), send(chunk(1, 0), 0, 1))
    return jnp.where(first, same, cross), jnp.where(first, cross, same)


def shards(diag_tiles, left_factors, right_factors, ranks):
    row_at = lax.axis_index("row")
    col_at = lax.axis_index("col")
    z, core = col_at // 2, col_at % 2
    place = jnp.stack([z, core, row_at]).astype(jnp.int32)
    mine = diag_tiles[0, 0]
    keep = jnp.arange(RANK)[None, :] < ranks[0, 0, 0, 0]
    zero = jnp.zeros((), BF16)
    both = jnp.concatenate(
        [jnp.where(keep, left_factors[0, 0, 0, 0], zero), jnp.where(keep, right_factors[0, 0, 0, 0], zero)], axis=1
    )

    band = lax.dynamic_slice(jnp.concatenate([mine, mine[:, :BAND]], axis=1), (0, BLK * z), (64, BAND))
    half_way = spread_x(band, row_at, (0, 1))
    half = halve(after(both, half_way), z, 4)
    band0, band1 = spread_y(half_way, row_at, (0, 1))
    raw0 = lax.all_gather(band0, "col", tiled=True)

    quarter = halve(after(half, band0), z, 2)
    part0, part1 = deal(quarter, z, core, ())
    first = spread_x(part0, row_at, (1,))
    flip = lax.ppermute(
        jnp.concatenate([part0[:, RANK:], part1[:, RANK:]], axis=1),
        ("row", "col"),
        [(at(r, c), at(c, r)) for r in range(16) for c in range(16)],
    )
    first, flip = lax.optimization_barrier((first, flip))
    (first,) = spread_y(first, row_at, (1,))
    hi, lo = split(band1)
    tile = lax.all_gather(jnp.concatenate([hi, lo, first, part0, part1], axis=1), "col", tiled=True)
    over_x = [
        lax.ppermute(flip, "row", [(4 * a + b, 4 * ((a + s) % 4) + b) for a in range(4) for b in range(4)])
        for s in (1, 2, 3)
    ]

    lrow0, lb0, mh0, ml0 = pl.pallas_call(
        first_kernel,
        out_shape=FACTOR,
        in_specs=[SMEM, ANY],
        out_specs=[VMEM] * 4,
        scratch_shapes=[
            pltpu.VMEM((NB, BAND), F32),
            pltpu.VMEM((NB, NB), F32),
            pltpu.VMEM((BLK, BLK), F32),
            pltpu.SemaphoreType.DMA((1,)),
        ],
        compiler_params=grant(56),
        name="factor_first",
    )(place, raw0)

    parts = [jnp.concatenate(lax.optimization_barrier((flip, *over_x, mh0))[:4], axis=0)]
    for s in (1, 2, 3):
        parts.append(
            lax.ppermute(parts[0], "row", [(4 * a + b, 4 * a + (b + s) % 4) for a in range(4) for b in range(4)])
        )

    lrow1, lb1, mh1, ml1, p10i = pl.pallas_call(
        second_kernel,
        out_shape=FACTOR + [shape(NB, 2 * RANK, BF16)],
        in_specs=[SMEM] + [ANY] * 4,
        out_specs=[VMEM] * 5,
        scratch_shapes=[
            pltpu.VMEM((NB, TILE1 + 2 * RANK), BF16),
            pltpu.VMEM((NB, NB), BF16),
            pltpu.VMEM((NB, BLK), BF16),
            pltpu.VMEM((NB, BLK), BF16),
            pltpu.VMEM((NB, NB), F32),
            pltpu.VMEM((NB, 2 * RANK), F32),
            pltpu.VMEM((BLK, BLK), F32),
            pltpu.SemaphoreType.DMA((4,)),
        ],
        compiler_params=grant(56),
        name="factor_second",
    )(place, tile, lb0, mh0, ml0)
    new, upd = pl.pallas_call(
        last_kernel,
        out_shape=[shape(64, NB, F32), shape(NB, 3 * RANK, BF16)],
        in_specs=[SMEM] + [ANY] * 15,
        out_specs=[VMEM] * 2,
        scratch_shapes=[
            pltpu.VMEM((NB, 2 * RANK), BF16),
            pltpu.VMEM((NB, 4 * RANK), BF16),
            pltpu.VMEM((NB, RANK), BF16),
            pltpu.VMEM((NB, 2 * RANK), BF16),
            pltpu.VMEM((64, NB), F32),
            pltpu.VMEM((64, NB), F32),
            pltpu.VMEM((64, NB), F32),
            pltpu.VMEM((NB, NB), BF16),
            pltpu.VMEM((NB, BLK), BF16),
            pltpu.VMEM((NB, BLK), BF16),
            pltpu.VMEM((NB, NB), BF16),
            pltpu.VMEM((NB, BLK), BF16),
            pltpu.VMEM((NB, BLK), BF16),
            pltpu.VMEM((NB, RANK), F32),
            pltpu.VMEM((NB, 3 * RANK), F32),
            pltpu.VMEM((NB, RANK), BF16),
            pltpu.VMEM((NB, 3 * RANK), BF16),
            pltpu.SemaphoreType.DMA((28,)),
        ],
        compiler_params=grant(56),
        name="finish",
    )(place, *parts, tile, p10i, mine, lrow0, lrow1, lb0, mh0, ml0, lb1, mh1, ml1)
    return new[None, None], upd[None, None, None, None]


def solution(mesh):
    in_specs = (
        P(None, "row", "col", None),
        P(None, "row", None, "col", None, None),
        P(None, "row", None, "col", None, None),
        P(None, "row", None, "col"),
    )
    out_specs = (P(None, "row", "col", None), P(None, "row", None, "col", None, None))
    return jax.shard_map(shards, mesh=mesh, in_specs=in_specs, out_specs=out_specs, check_vma=False)
```

profile of v0, /device:TPU:1, one launch (start us, length us, event | category | flops | bytes accessed | tf_op | source)
XLA Modules:
  0.0 207.4 jit_solution(10885132751255371234)
XLA Ops:
  7.2 0.0 all-gather.3.cloned.1.call-start
  7.2 1.0 slice.48
  8.3 0.9 fusion
  9.2 4.0 %collective-permute-start.2 = (f32[64,640]{1,0:T(8,128)S(1)}, f32[64,640]{1,0:T(8,128)S(1)}, u32[]{:S(2)}, u32[]{:S(2)}) collective-permute-start(f32[64,640]{1,0:T(8,128)S(1)} %fusion), channel_id=1, source_target_pairs={{0,64},{16,80},{1,65},{17,81},{2,66},{18,82},{3,67},{19,83},{4,68}... | collective-permute-start | bytes 491528 | tf_op jit(solution)/shard_map/ppermute | solution.py:313
  13.2 2.2 %collective-permute-start.1 = (f32[64,640]{1,0:T(8,128)S(1)}, f32[64,640]{1,0:T(8,128)S(1)}, u32[]{:S(2)}, u32[]{:S(2)}) collective-permute-start(f32[64,640]{1,0:T(8,128)S(1)} %fusion), channel_id=1, source_target_pairs={{0,128},{16,144},{1,129},{17,145},{2,130},{18,146},{3,131},{19,147... | collective-permute-start | bytes 491528 | tf_op jit(solution)/shard_map/ppermute | solution.py:313
  15.4 1.3 collective-permute-start
  16.7 0.0 collective-permute-done.2
  16.7 2.8 %collective-permute-done.1 = f32[64,640]{1,0:T(8,128)S(1)} collective-permute-done((f32[64,640]{1,0:T(8,128)S(1)}, f32[64,640]{1,0:T(8,128)S(1)}, u32[]{:S(2)}, u32[]{:S(2)}) %collective-permute-start.1) | collective-permute-done | bytes 163872 | tf_op jit(solution)/shard_map/ppermute | solution.py:313
  19.5 0.0 collective-permute-done
  19.6 3.2 %collective-permute-start.6 = (f32[64,640]{1,0:T(8,128)S(1)}, f32[64,640]{1,0:T(8,128)S(1)}, u32[]{:S(2)}, u32[]{:S(2)}) collective-permute-start(f32[64,640]{1,0:T(8,128)S(1)} %select_select_fusion.2), channel_id=1, source_target_pairs={{0,16},{16,32},{64,80},{80,96},{128,144},{144,160},{192,208},{208,... | collective-permute-start | bytes 491528 | tf_op jit(solution)/shard_map/ppermute | solution.py:318
  22.8 1.3 collective-permute-start.5
  24.1 1.9 collective-permute-start.4
  26.0 0.0 collective-permute-done.6
  26.0 2.2 %collective-permute-done.5 = f32[64,640]{1,0:T(8,128)S(1)} collective-permute-done((f32[64,640]{1,0:T(8,128)S(1)}, f32[64,640]{1,0:T(8,128)S(1)}, u32[]{:S(2)}, u32[]{:S(2)}) %collective-permute-start.5) | collective-permute-done | bytes 163872 | tf_op jit(solution)/shard_map/ppermute | solution.py:318
  28.2 2.3 %collective-permute-done.4 = f32[64,640]{1,0:T(8,128)S(1)} collective-permute-done((f32[64,640]{1,0:T(8,128)S(1)}, f32[64,640]{1,0:T(8,128)S(1)}, u32[]{:S(2)}, u32[]{:S(2)}) %collective-permute-start.4) | collective-permute-done | bytes 163872 | tf_op jit(solution)/shard_map/ppermute | solution.py:318
  30.5 0.7 select_select_fusion.1
  31.2 0.0 all-gather.3.cloned.1.call-update
  31.3 0.0 all-gather.5.cloned.1.call-start
  32.0 0.1 bitcast_select_fusion.1
  32.1 0.1 pad_maximum_fusion
  32.2 8.8 %collective-permute-start.3 = (bf16[512,512]{1,0:T(8,128)(2,1)S(1)}, bf16[512,512]{1,0:T(8,128)(2,1)S(1)}, u32[]{:S(2)}, u32[]{:S(2)}) collective-permute-start(bf16[512,512]{1,0:T(8,128)(2,1)S(1)} %slice.38), channel_id=1, source_target_pairs={{0,8},{1,9},{16,24},{17,25},{32,40},{33,41},{48,56},{49,57},{64,72... | collective-permute-start | bytes 1572872 | tf_op jit(solution)/shard_map/ppermute | solution.py:325
  41.1 10.3 %collective-permute-done.3 = bf16[512,512]{1,0:T(8,128)(2,1)S(1)} collective-permute-done((bf16[512,512]{1,0:T(8,128)(2,1)S(1)}, bf16[512,512]{1,0:T(8,128)(2,1)S(1)}, u32[]{:S(2)}, u32[]{:S(2)}) %collective-permute-start.3) | collective-permute-done | bytes 524320 | tf_op jit(solution)/shard_map/ppermute | solution.py:325
  51.4 0.1 slice_select_fusion
  51.5 1.3 collective-permute-start.7
  52.8 10.3 %collective-permute-done.7 = bf16[256,512]{1,0:T(8,128)(2,1)S(1)} collective-permute-done((bf16[256,512]{1,0:T(8,128)(2,1)S(1)}, bf16[256,512]{1,0:T(8,128)(2,1)S(1)}, u32[]{:S(2)}, u32[]{:S(2)}) %collective-permute-start.7) | collective-permute-done | bytes 262176 | tf_op jit(solution)/shard_map/ppermute | solution.py:325
  63.2 1.3 collective-permute-start.9
  64.5 1.3 collective-permute-start.8
  65.8 9.7 %collective-permute-start.10 = (bf16[64,512]{1,0:T(8,128)(2,1)S(1)}, bf16[64,512]{1,0:T(8,128)(2,1)S(1)}, u32[]{:S(2)}, u32[]{:S(2)}) collective-permute-start(bf16[64,512]{1,0:T(8,128)(2,1)S(1)} %get-tuple-element.46), channel_id=1, source_target_pairs={{0,1},{1,0},{4,5},{5,4},{8,9},{9,8},{12,13},{13,12},{16,17},{17,16... | collective-permute-start | bytes 196616 | tf_op jit(solution)/shard_map/ppermute | solution.py:337
  75.5 0.0 collective-permute-done.9
  75.5 0.0 collective-permute-done.8
  75.5 0.8 collective-permute-done.10
  76.4 0.7 collective-permute-start.13
  77.1 0.7 collective-permute-start.12
  77.7 0.7 collective-permute-start.11
  78.4 7.1 %collective-permute-start.14 = (bf16[64,512]{1,0:T(8,128)(2,1)S(1)}, bf16[64,512]{1,0:T(8,128)(2,1)S(1)}, u32[]{:S(2)}, u32[]{:S(2)}) collective-permute-start(bf16[64,512]{1,0:T(8,128)(2,1)S(1)} %pad_maximum_fusion.1), channel_id=1, source_target_pairs={{0,0},{1,16},{2,32},{3,48},{4,64},{5,80},{6,96},{7,112},{8,128},{9... | collective-permute-start | bytes 196616 | tf_op jit(solution)/shard_map/ppermute | solution.py:366
  85.5 0.0 collective-permute-done.13
  85.5 0.0 collective-permute-done.12
  85.6 0.0 collective-permute-done.11
  85.6 1.9 collective-permute-done.14
  87.5 0.7 collective-permute-start.23
  88.2 0.7 collective-permute-start.22
  88.8 1.3 collective-permute-start.21
  90.2 0.0 collective-permute-done.22
  90.2 8.7 %collective-permute-done.21 = bf16[64,512]{1,0:T(8,128)(2,1)S(1)} collective-permute-done((bf16[64,512]{1,0:T(8,128)(2,1)S(1)}, bf16[64,512]{1,0:T(8,128)(2,1)S(1)}, u32[]{:S(2)}, u32[]{:S(2)}) %collective-permute-start.21) | collective-permute-done | bytes 65568 | tf_op jit(solution)/shard_map/ppermute | solution.py:318
  99.0 0.0 copy-start
  99.0 0.7 copy-done
  99.7 0.0 all-gather.5.cloned.1.call-update
  99.7 8.1 %collective-permute-start.17 = (bf16[64,512]{1,0:T(8,128)(2,1)S(1)}, bf16[64,512]{1,0:T(8,128)(2,1)S(1)}, u32[]{:S(2)}, u32[]{:S(2)}) collective-permute-start(bf16[64,512]{1,0:T(8,128)(2,1)S(1)} %collective-permute-done.14), channel_id=1, source_target_pairs={{0,192},{16,208},{32,224},{48,240},{64,0},{80,16},{96,32},{112,48}... | collective-permute-start | bytes 196616 | tf_op jit(solution)/shard_map/ppermute | solution.py:376
  107.9 0.7 collective-permute-start.15
  108.5 0.6 pad_add_fusion.place
  109.1 28.1 %factor_first.1 = (f32[64,1024]{1,0:T(8,128)}, bf16[1024,1024]{1,0:T(8,128)(2,1)}, bf16[1024,128]{1,0:T(8,128)(2,1)}, bf16[1024,128]{1,0:T(8,128)(2,1)}) custom-call(s32[3]{0:T(128)} %pad_add_fusion.place, f32[1024,640]{1,0:T(8,128)} %all-gather.3.cloned.1.call-done.raw_h), custom_call_target="tpu_custom_call" | custom-call | tf_op jit(solution)/shard_map/factor_first/pallas_call | solution.py:380
  137.2 0.0 collective-permute-done.16
  137.2 0.0 collective-permute-done.15
  137.3 1.5 collective-permute-start.20
  138.8 0.0 collective-permute-start.19
  138.8 0.9 collective-permute-start.18
  139.7 8.0 %all-gather.5.cloned.1.call-done.tile_h.refs_4_ = bf16[1024,2816]{1,0:T(8,128)(2,1)} async-done(((bf16[64,2816]{1,0:T(8,128)(2,1)}), bf16[1024,2816]{1,0:T(8,128)(2,1)}) %all-gather.5.cloned.1.call-update) | async-done | bytes 5767184 | tf_op jit(solution)/shard_map/all_gather | solution.py:374
  147.7 35.7 %factor_second.1 = (f32[64,1024]{1,0:T(8,128)}, bf16[1024,1024]{1,0:T(8,128)(2,1)}, bf16[1024,128]{1,0:T(8,128)(2,1)}, bf16[1024,128]{1,0:T(8,128)(2,1)}, bf16[1024,512]{1,0:T(8,128)(2,1)}) custom-call(s32[3]{0:T(128)} %pad_add_fusion.place, bf16[1024,2816]{1,0:T(8,128)(2,1)} %all-gather.5.cloned.1.call-done.tile_h.refs_4_, ...), custom_call_target="tpu_custom_call" | custom-call | tf_op jit(solution)/shard_map/factor_second/pallas_call | solution.py:401
  183.4 0.0 collective-permute-done.20.refs_3_
  183.4 0.0 collective-permute-done.19.refs_2_
  183.5 0.7 copy-done.4
  184.1 0.1 copy-done.5
  184.3 0.0 copy-done.6
  184.3 16.2 %finish.1 = (f32[64,1024]{1,0:T(8,128)}, bf16[1024,768]{1,0:T(8,128)(2,1)}) custom-call(s32[3]{0:T(128)} %pad_add_fusion.place, bf16[256,512]{1,0:T(8,128)(2,1)} %copy-done.3, bf16[256,512]{1,0:T(8,128)(2,1)} %copy-done.6, bf16[256,512]{1,0:T(8,128)(2,1)} %copy-done.5, bf16[256,512]{1,0:T(8,128)(2,1)} %copy-done.4, ...), custom_call_target="tpu_custom_call" | custom-call | tf_op jit(solution)/shard_map/finish/pallas_call | solution.py:419
  (34 shorter events, 0.4 us)
Async XLA Ops:
  7.2 24.8 %copy-start.2 = (bf16[1,1,1,1,1024,256]{5,4,3,2,1,0:T(8,128)(2,1)S(1)}, bf16[1,1,1,1,1024,256]{5,4,3,2,1,0:T(8,128)(2,1)}, u32[]{:S(2)}) copy-start(bf16[1,1,1,1,1024,256]{5,4,3,2,1,0:T(8,128)(2,1)} %param.6) | copy-start | bytes 1572868
  7.2 24.8 %copy-start.1 = (bf16[1,1,1,1,1024,256]{5,4,3,2,1,0:T(8,128)(2,1)S(1)}, bf16[1,1,1,1,1024,256]{5,4,3,2,1,0:T(8,128)(2,1)}, u32[]{:S(2)}) copy-start(bf16[1,1,1,1,1024,256]{5,4,3,2,1,0:T(8,128)(2,1)} %param.5) | copy-start | bytes 1572868
  7.2 101.9 %all-gather.3.cloned.1.call-start = ((), (), s32[]{:S(2)}) async-start(), calls=%async_computation | async-start | bytes 2785280 | tf_op jit(solution)/shard_map/all_gather | solution.py:361
  9.2 7.5 %collective-permute-start.2 = (f32[64,640]{1,0:T(8,128)S(1)}, f32[64,640]{1,0:T(8,128)S(1)}, u32[]{:S(2)}, u32[]{:S(2)}) collective-permute-start(f32[64,640]{1,0:T(8,128)S(1)} %fusion), channel_id=1, source_target_pairs={{0,64},{16,80},{1,65},{17,81},{2,66},{18,82},{3,67},{19,83},{4,68}... | collective-permute-start | bytes 491528 | tf_op jit(solution)/shard_map/ppermute | solution.py:313
  13.2 6.4 %collective-permute-start.1 = (f32[64,640]{1,0:T(8,128)S(1)}, f32[64,640]{1,0:T(8,128)S(1)}, u32[]{:S(2)}, u32[]{:S(2)}) collective-permute-start(f32[64,640]{1,0:T(8,128)S(1)} %fusion), channel_id=1, source_target_pairs={{0,128},{16,144},{1,129},{17,145},{2,130},{18,146},{3,131},{19,147... | collective-permute-start | bytes 491528 | tf_op jit(solution)/shard_map/ppermute | solution.py:313
  15.4 4.1 %collective-permute-start = (f32[64,640]{1,0:T(8,128)S(1)}, f32[64,640]{1,0:T(8,128)S(1)}, u32[]{:S(2)}, u32[]{:S(2)}) collective-permute-start(f32[64,640]{1,0:T(8,128)S(1)} %fusion), channel_id=1, source_target_pairs={{0,192},{16,208},{1,193},{17,209},{2,194},{18,210},{3,195},{19,211... | collective-permute-start | bytes 491528 | tf_op jit(solution)/shard_map/ppermute | solution.py:313
  19.6 6.5 %collective-permute-start.6 = (f32[64,640]{1,0:T(8,128)S(1)}, f32[64,640]{1,0:T(8,128)S(1)}, u32[]{:S(2)}, u32[]{:S(2)}) collective-permute-start(f32[64,640]{1,0:T(8,128)S(1)} %select_select_fusion.2), channel_id=1, source_target_pairs={{0,16},{16,32},{64,80},{80,96},{128,144},{144,160},{192,208},{208,... | collective-permute-start | bytes 491528 | tf_op jit(solution)/shard_map/ppermute | solution.py:318
  22.8 5.4 %collective-permute-start.5 = (f32[64,640]{1,0:T(8,128)S(1)}, f32[64,640]{1,0:T(8,128)S(1)}, u32[]{:S(2)}, u32[]{:S(2)}) collective-permute-start(f32[64,640]{1,0:T(8,128)S(1)} %select_select_fusion.2), channel_id=1, source_target_pairs={{0,32},{16,48},{64,96},{80,112},{128,160},{144,176},{192,224},{208... | collective-permute-start | bytes 491528 | tf_op jit(solution)/shard_map/ppermute | solution.py:318
  24.1 6.5 %collective-permute-start.4 = (f32[64,640]{1,0:T(8,128)S(1)}, f32[64,640]{1,0:T(8,128)S(1)}, u32[]{:S(2)}, u32[]{:S(2)}) collective-permute-start(f32[64,640]{1,0:T(8,128)S(1)} %select_select_fusion.2), channel_id=1, source_target_pairs={{0,48},{16,0},{64,112},{80,64},{128,176},{144,128},{192,240},{208,... | collective-permute-start | bytes 491528 | tf_op jit(solution)/shard_map/ppermute | solution.py:318
  31.3 116.4 %all-gather.5.cloned.1.call-start = ((), (), s32[]{:S(2)}) async-start(), calls=%async_computation.1 | async-start | bytes 6127616 | tf_op jit(solution)/shard_map/all_gather | solution.py:374
  32.2 19.2 %collective-permute-start.3 = (bf16[512,512]{1,0:T(8,128)(2,1)S(1)}, bf16[512,512]{1,0:T(8,128)(2,1)S(1)}, u32[]{:S(2)}, u32[]{:S(2)}) collective-permute-start(bf16[512,512]{1,0:T(8,128)(2,1)S(1)} %slice.38), channel_id=1, source_target_pairs={{0,8},{1,9},{16,24},{17,25},{32,40},{33,41},{48,56},{49,57},{64,72... | collective-permute-start | bytes 1572872 | tf_op jit(solution)/shard_map/ppermute | solution.py:325
  51.5 11.7 %collective-permute-start.7 = (bf16[256,512]{1,0:T(8,128)(2,1)S(1)}, bf16[256,512]{1,0:T(8,128)(2,1)S(1)}, u32[]{:S(2)}, u32[]{:S(2)}) collective-permute-start(bf16[256,512]{1,0:T(8,128)(2,1)S(1)} %slice.40), channel_id=1, source_target_pairs={{0,4},{1,5},{8,12},{9,13},{16,20},{17,21},{24,28},{25,29},{32,36},... | collective-permute-start | bytes 786440 | tf_op jit(solution)/shard_map/ppermute | solution.py:325
  63.2 12.4 %collective-permute-start.9 = (bf16[64,512]{1,0:T(8,128)(2,1)S(1)}, bf16[64,512]{1,0:T(8,128)(2,1)S(1)}, u32[]{:S(2)}, u32[]{:S(2)}) collective-permute-start(bf16[64,512]{1,0:T(8,128)(2,1)S(1)} %get-tuple-element.45), channel_id=1, source_target_pairs={{0,3},{1,2},{4,7},{5,6},{8,11},{9,10},{12,15},{13,14},{16,19},{17,... | collective-permute-start | bytes 196616 | tf_op jit(solution)/shard_map/ppermute | solution.py:337
  64.5 11.1 %collective-permute-start.8 = (bf16[64,512]{1,0:T(8,128)(2,1)S(1)}, bf16[64,512]{1,0:T(8,128)(2,1)S(1)}, u32[]{:S(2)}, u32[]{:S(2)}) collective-permute-start(bf16[64,512]{1,0:T(8,128)(2,1)S(1)} %get-tuple-element.44), channel_id=1, source_target_pairs={{0,2},{1,3},{4,6},{5,7},{8,10},{9,11},{12,14},{13,15},{16,18},{17,... | collective-permute-start | bytes 196616 | tf_op jit(solution)/shard_map/ppermute | solution.py:337
  65.8 10.6 %collective-permute-start.10 = (bf16[64,512]{1,0:T(8,128)(2,1)S(1)}, bf16[64,512]{1,0:T(8,128)(2,1)S(1)}, u32[]{:S(2)}, u32[]{:S(2)}) collective-permute-start(bf16[64,512]{1,0:T(8,128)(2,1)S(1)} %get-tuple-element.46), channel_id=1, source_target_pairs={{0,1},{1,0},{4,5},{5,4},{8,9},{9,8},{12,13},{13,12},{16,17},{17,16... | collective-permute-start | bytes 196616 | tf_op jit(solution)/shard_map/ppermute | solution.py:337
  76.4 9.1 %collective-permute-start.13 = (bf16[64,512]{1,0:T(8,128)(2,1)S(1)}, bf16[64,512]{1,0:T(8,128)(2,1)S(1)}, u32[]{:S(2)}, u32[]{:S(2)}) collective-permute-start(bf16[64,512]{1,0:T(8,128)(2,1)S(1)} %get-tuple-element.43), channel_id=1, source_target_pairs={{16,80},{17,81},{18,82},{19,83},{20,84},{21,85},{22,86},{23,87},{2... | collective-permute-start | bytes 196616 | tf_op jit(solution)/shard_map/ppermute | solution.py:313
  77.1 8.5 %collective-permute-start.12 = (bf16[64,512]{1,0:T(8,128)(2,1)S(1)}, bf16[64,512]{1,0:T(8,128)(2,1)S(1)}, u32[]{:S(2)}, u32[]{:S(2)}) collective-permute-start(bf16[64,512]{1,0:T(8,128)(2,1)S(1)} %get-tuple-element.43), channel_id=1, source_target_pairs={{16,144},{17,145},{18,146},{19,147},{20,148},{21,149},{22,150},{23... | collective-permute-start | bytes 196616 | tf_op jit(solution)/shard_map/ppermute | solution.py:313
  77.7 7.8 %collective-permute-start.11 = (bf16[64,512]{1,0:T(8,128)(2,1)S(1)}, bf16[64,512]{1,0:T(8,128)(2,1)S(1)}, u32[]{:S(2)}, u32[]{:S(2)}) collective-permute-start(bf16[64,512]{1,0:T(8,128)(2,1)S(1)} %get-tuple-element.43), channel_id=1, source_target_pairs={{16,208},{17,209},{18,210},{19,211},{20,212},{21,213},{22,214},{23... | collective-permute-start | bytes 196616 | tf_op jit(solution)/shard_map/ppermute | solution.py:313
  78.4 9.0 %collective-permute-start.14 = (bf16[64,512]{1,0:T(8,128)(2,1)S(1)}, bf16[64,512]{1,0:T(8,128)(2,1)S(1)}, u32[]{:S(2)}, u32[]{:S(2)}) collective-permute-start(bf16[64,512]{1,0:T(8,128)(2,1)S(1)} %pad_maximum_fusion.1), channel_id=1, source_target_pairs={{0,0},{1,16},{2,32},{3,48},{4,64},{5,80},{6,96},{7,112},{8,128},{9... | collective-permute-start | bytes 196616 | tf_op jit(solution)/shard_map/ppermute | solution.py:366
  87.5 2.7 %collective-permute-start.23 = (bf16[64,512]{1,0:T(8,128)(2,1)S(1)}, bf16[64,512]{1,0:T(8,128)(2,1)S(1)}, u32[]{:S(2)}, u32[]{:S(2)}) collective-permute-start(bf16[64,512]{1,0:T(8,128)(2,1)S(1)} %select_select_fusion.3), channel_id=1, source_target_pairs={{16,32},{80,96},{144,160},{208,224},{17,33},{81,97},{145,161},{209... | collective-permute-start | bytes 196616 | tf_op jit(solution)/shard_map/ppermute | solution.py:318
  88.2 2.0 collective-permute-start.22
  88.8 10.1 %collective-permute-start.21 = (bf16[64,512]{1,0:T(8,128)(2,1)S(1)}, bf16[64,512]{1,0:T(8,128)(2,1)S(1)}, u32[]{:S(2)}, u32[]{:S(2)}) collective-permute-start(bf16[64,512]{1,0:T(8,128)(2,1)S(1)} %select_select_fusion.3), channel_id=1, source_target_pairs={{16,0},{80,64},{144,128},{208,192},{17,1},{81,65},{145,129},{209,1... | collective-permute-start | bytes 196616 | tf_op jit(solution)/shard_map/ppermute | solution.py:318
  99.0 0.7 copy-start
  99.7 37.5 %collective-permute-start.17 = (bf16[64,512]{1,0:T(8,128)(2,1)S(1)}, bf16[64,512]{1,0:T(8,128)(2,1)S(1)}, u32[]{:S(2)}, u32[]{:S(2)}) collective-permute-start(bf16[64,512]{1,0:T(8,128)(2,1)S(1)} %collective-permute-done.14), channel_id=1, source_target_pairs={{0,192},{16,208},{32,224},{48,240},{64,0},{80,16},{96,32},{112,48}... | collective-permute-start | bytes 196616 | tf_op jit(solution)/shard_map/ppermute | solution.py:376
  107.9 29.3 %collective-permute-start.16 = (bf16[64,512]{1,0:T(8,128)(2,1)S(1)}, bf16[64,512]{1,0:T(8,128)(2,1)S(1)}, u32[]{:S(2)}, u32[]{:S(2)}) collective-permute-start(bf16[64,512]{1,0:T(8,128)(2,1)S(1)} %collective-permute-done.14), channel_id=1, source_target_pairs={{0,128},{16,144},{32,160},{48,176},{64,192},{80,208},{96,224},{112... | collective-permute-start | bytes 196616 | tf_op jit(solution)/shard_map/ppermute | solution.py:376
  107.9 29.4 %collective-permute-start.15 = (bf16[64,512]{1,0:T(8,128)(2,1)S(1)}, bf16[64,512]{1,0:T(8,128)(2,1)S(1)}, u32[]{:S(2)}, u32[]{:S(2)}) collective-permute-start(bf16[64,512]{1,0:T(8,128)(2,1)S(1)} %collective-permute-done.14), channel_id=1, source_target_pairs={{0,64},{16,80},{32,96},{48,112},{64,128},{80,144},{96,160},{112,17... | collective-permute-start | bytes 196616 | tf_op jit(solution)/shard_map/ppermute | solution.py:376
  137.3 46.1 %copy-start.3 = (bf16[256,512]{1,0:T(8,128)(2,1)}, bf16[256,512]{1,0:T(8,128)(2,1)S(1)}, u32[]{:S(2)}) copy-start(bf16[256,512]{1,0:T(8,128)(2,1)S(1)} %constant_dynamic-update-slice_fusion.refs_0_) | copy-start | bytes 786436
  137.3 46.1 %collective-permute-start.20 = (bf16[256,512]{1,0:T(8,128)(2,1)S(1)}, bf16[256,512]{1,0:T(8,128)(2,1)S(1)}, u32[]{:S(2)}, u32[]{:S(2)}) collective-permute-start(bf16[256,512]{1,0:T(8,128)(2,1)S(1)} %constant_dynamic-update-slice_fusion.refs_0_), channel_id=1, source_target_pairs={{0,48},{16,0},{32,16},{48,32},{64,112},{80,64},{96,80},{112,96},{1... | collective-permute-start | bytes 786440 | tf_op jit(solution)/shard_map/ppermute | solution.py:398
  138.8 44.6 %collective-permute-start.19 = (bf16[256,512]{1,0:T(8,128)(2,1)S(1)}, bf16[256,512]{1,0:T(8,128)(2,1)S(1)}, u32[]{:S(2)}, u32[]{:S(2)}) collective-permute-start(bf16[256,512]{1,0:T(8,128)(2,1)S(1)} %constant_dynamic-update-slice_fusion.refs_0_), channel_id=1, source_target_pairs={{0,32},{16,48},{32,0},{48,16},{64,96},{80,112},{96,64},{112,80},{1... | collective-permute-start | bytes 786440 | tf_op jit(solution)/shard_map/ppermute | solution.py:398
  138.8 44.7 %collective-permute-start.18 = (bf16[256,512]{1,0:T(8,128)(2,1)S(1)}, bf16[256,512]{1,0:T(8,128)(2,1)S(1)}, u32[]{:S(2)}, u32[]{:S(2)}) collective-permute-start(bf16[256,512]{1,0:T(8,128)(2,1)S(1)} %constant_dynamic-update-slice_fusion.refs_0_), channel_id=1, source_target_pairs={{0,16},{16,32},{32,48},{48,0},{64,80},{80,96},{96,112},{112,64},{1... | collective-permute-start | bytes 786440 | tf_op jit(solution)/shard_map/ppermute | solution.py:398
  183.4 0.7 copy-start.4
  183.5 0.8 copy-start.5
  183.5 0.8 copy-start.6
Sparse Core Ops, SparseCore 0:
  31.4 46.7 all-gather.2
  99.8 47.7 all-gather.4
where the time goes:
time: 208 us; the launch traced here: 207 us
  Pallas kernels  80 us (38%)
  starting transfers between devices  59.3 us (29%)
  waiting for transfers between devices  47.4 us (23%)
  between operations  15.4 us (7%)
  local copies, waits for them, and re-layouts  2.68 us (1%)
  other arithmetic  2.67 us (1%)
    pallas_call x1, Pallas kernels, shards(): pl.pallas_call(second_kernel, out_shape=FACTOR + [shape(NB, 2 * RANK, BF1...  35.7 us
    pallas_call x1, Pallas kernels, shards(): pl.pallas_call(first_kernel, out_shape=FACTOR, in_specs=[SMEM, ANY], out_...  28.1 us
    ppermute x2, waiting for transfers between devices, halve(): got = lax.ppermute(x[half:], 'col', pairs)  20.6 us
    pallas_call x1, Pallas kernels, shards(): pl.pallas_call(last_kernel, out_shape=[shape(64, NB, F32), shape(NB, 3 *...  16.2 us
    ppermute x6, waiting for transfers between devices, spread_y(): lax.ppermute(x, 'row', [(4 * a + y, 4 * a + (y + s) % 4) for a in range(4...  13.2 us
    ppermute x3, starting transfers between devices, send(): return lax.ppermute(after(x, *tokens), 'col', pairs)  12.3 us
    ppermute x2, starting transfers between devices, halve(): got = lax.ppermute(x[half:], 'col', pairs)  10.1 us
    ppermute x6, starting transfers between devices, spread_x(): lax.ppermute(x, 'row', [(y, 4 * k + y) for y in rows])  9.45 us
  transfers between devices with their start and end apart: 26, of which 9 were waited for; matrix products, arithmetic and copies ran while one was open for 1% of the time, Pallas kernels for 31%

commit v1 on v0

--- a/solution.py
+++ b/solution.py
@@ -200,8 +200,18 @@
 def second_kernel(
     place, tile_h, lb0_h, mh0_h, ml0_h, lrow, lb, mh, ml, p10, tile, lb0, mh0, ml0, work, w, inv_s, sems
 ):
-    copies = fetch([(tile_h.at[:, : TILE1 + 2 * RANK], tile), (mh0_h, mh0), (ml0_h, ml0), (lb0_h, lb0)], sems)
-    for one in copies:
+    diag, factors = pl.ds(0, 2 * BAND), pl.ds(2 * BAND, 4 * RANK)
+    copies = fetch(
+        [
+            (tile_h.at[:, factors], tile.at[:, factors]),
+            (mh0_h, mh0),
+            (ml0_h, ml0),
+            (lb0_h, lb0),
+            (tile_h.at[:, diag], tile.at[:, diag]),
+        ],
+        sems,
+    )
+    for one in copies[:4]:
         one.wait()
     w[:, :RANK] = tile[:, 2 * BAND + RANK : TILE1].astype(F32)
     w[:, RANK:] = tile[:, TILE1 + RANK : TILE1 + 2 * RANK].astype(F32)
@@ -216,6 +226,7 @@
         rows = slice(r * BLK, (r + 1) * BLK)
         return tile[rows, cols].astype(F32) + tile[rows, cols.start + BAND : cols.stop + BAND].astype(F32)
 
+    copies[4].wait()
     unfold(work, take)
     for r in range(NBLK):
         o = r * BLK
@@ -355,27 +366,20 @@
     )
 
     band = lax.dynamic_slice(jnp.concatenate([mine, mine[:, :BAND]], axis=1), (0, BLK * z), (64, BAND))
-    half_way = spread_x(band, row_at, (0, 1))
-    half = halve(after(both, half_way), z, 4)
-    band0, band1 = spread_y(half_way, row_at, (0, 1))
+    half = halve(both, z, 4)
+    band0, band1 = spread_y(spread_x(band, row_at, (0, 1)), row_at, (0, 1))
+    band0, half = lax.optimization_barrier((band0, half))
     raw0 = lax.all_gather(band0, "col", tiled=True)
 
-    quarter = halve(after(half, band0), z, 2)
-    part0, part1 = deal(quarter, z, core, ())
-    first = spread_x(part0, row_at, (1,))
+    part0, part1 = deal(halve(half, z, 2), z, core, ())
+    (first,) = spread_y(spread_x(part0, row_at, (1,)), row_at, (1,))
+    hi, lo = split(band1)
+    tile = lax.all_gather(jnp.concatenate([hi, lo, first, part0, part1], axis=1), "col", tiled=True)
     flip = lax.ppermute(
-        jnp.concatenate([part0[:, RANK:], part1[:, RANK:]], axis=1),
+        after(jnp.concatenate([part0[:, RANK:], part1[:, RANK:]], axis=1), first),
         ("row", "col"),
         [(at(r, c), at(c, r)) for r in range(16) for c in range(16)],
     )
-    first, flip = lax.optimization_barrier((first, flip))
-    (first,) = spread_y(first, row_at, (1,))
-    hi, lo = split(band1)
-    tile = lax.all_gather(jnp.concatenate([hi, lo, first, part0, part1], axis=1), "col", tiled=True)
-    over_x = [
-        lax.ppermute(flip, "row", [(4 * a + b, 4 * ((a + s) % 4) + b) for a in range(4) for b in range(4)])
-        for s in (1, 2, 3)
-    ]
 
     lrow0, lb0, mh0, ml0 = pl.pallas_call(
         first_kernel,
@@ -392,7 +396,12 @@
         name="factor_first",
     )(place, raw0)
 
-    parts = [jnp.concatenate(lax.optimization_barrier((flip, *over_x, mh0))[:4], axis=0)]
+    flip = after(flip, mh0)
+    over_x = [
+        lax.ppermute(flip, "row", [(4 * a + b, 4 * ((a + s) % 4) + b) for a in range(4) for b in range(4)])
+        for s in (1, 2, 3)
+    ]
+    parts = [jnp.concatenate([flip, *over_x], axis=0)]
     for s in (1, 2, 3):
         parts.append(
             lax.ppermute(parts[0], "row", [(4 * a + b, 4 * a + (b + s) % 4) for a in range(4) for b in range(4)])
@@ -411,7 +420,7 @@
             pltpu.VMEM((NB, NB), F32),
             pltpu.VMEM((NB, 2 * RANK), F32),
             pltpu.VMEM((BLK, BLK), F32),
-            pltpu.SemaphoreType.DMA((4,)),
+            pltpu.SemaphoreType.DMA((5,)),
         ],
         compiler_params=grant(56),
         name="factor_second",

time: 208 us -> 186 us (0.89)
  starting transfers between devices: 59.3 us -> 42 us
  waiting for transfers between devices: 47.4 us -> 41.9 us
    ppermute x2, waiting for transfers between devices: 20.6 us -> 3.83 us  [halve(): got = lax.ppermute(x[half:], 'col', pairs)]
    all_gather x1, waiting for transfers between devices: 0.01 us -> 13.8 us  [shards(): raw0 = lax.all_gather(band0, 'col', tiled=True)]
    ppermute x3, starting transfers between devices: 8.8 us -> 1.53 us  [shards(): lax.ppermute(flip, 'row', [(4 * a + b, 4 * ((a + s) % 4) + b) for a in ra...]
    ppermute x3, waiting for transfers between devices: 0.01 us -> 5.4 us  [shards(): lax.ppermute(flip, 'row', [(4 * a + b, 4 * ((a + s) % 4) + b) for a in ra...]
    ppermute x1, starting transfers between devices: 7.09 us -> 1.94 us  [shards(): lax.ppermute(after(jnp.concatenate([part0[:, RANK:], part1[:, RANK:]], ax...]
    ppermute x3, starting transfers between devices: 12.3 us -> 7.4 us  [send(): return lax.ppermute(after(x, *tokens), 'col', pairs)]
    ppermute x6, waiting for transfers between devices: 2.82 us -> 0.02 us  [spread_x(): lax.ppermute(x, 'row', [(y, 4 * k + y) for y in rows])]
    all_gather x1, waiting for transfers between devices: 7.99 us -> 5.88 us  [shards(): lax.all_gather(jnp.concatenate([hi, lo, first, part0, part1], axis=1), 'c...]
  transfers between devices with their start and end apart: 26 -> 26, of which waited for: 9 -> 8; matrix products, arithmetic and copies ran while one was open for 1% -> 2% of each run, Pallas kernels for 31% -> 34%
where the time goes in v1:
time: 186 us; the launch traced here: 185 us
  Pallas kernels  79.5 us (43%)
  starting transfers between devices  42 us (23%)
  waiting for transfers between devices  41.9 us (23%)
  between operations  15.4 us (8%)
  other arithmetic  4.01 us (2%)
  local copies, waits for them, and re-layouts  2.55 us (1%)
    pallas_call x1, Pallas kernels, shards(): pl.pallas_call(second_kernel, out_shape=FACTOR + [shape(NB, 2 * RANK, BF1...  35.2 us
    pallas_call x1, Pallas kernels, shards(): pl.pallas_call(first_kernel, out_shape=FACTOR, in_specs=[SMEM, ANY], out_...  28.1 us
    pallas_call x1, Pallas kernels, shards(): pl.pallas_call(last_kernel, out_shape=[shape(64, NB, F32), shape(NB, 3 *...  16.2 us
    all_gather x1, waiting for transfers between devices, shards(): raw0 = lax.all_gather(band0, 'col', tiled=True)  13.8 us
    ppermute x6, waiting for transfers between devices, spread_y(): lax.ppermute(x, 'row', [(4 * a + y, 4 * a + (y + s) % 4) for a in range(4...  12 us
    ppermute x2, starting transfers between devices, halve(): got = lax.ppermute(x[half:], 'col', pairs)  10.1 us
    ppermute x6, starting transfers between devices, spread_x(): lax.ppermute(x, 'row', [(y, 4 * k + y) for y in rows])  9.45 us
    ppermute x6, starting transfers between devices, spread_y(): lax.ppermute(x, 'row', [(4 * a + y, 4 * a + (y + s) % 4) for a in range(4...  9.05 us
  transfers between devices with their start and end apart: 26, of which 8 were waited for; matrix products, arithmetic and copies ran while one was open for 2% of the time, Pallas kernels for 34%

profile of v1, /device:TPU:1, one launch (start us, length us, event | category | flops | bytes accessed | tf_op | source)
XLA Modules:
  0.0 185.2 jit_solution(17167421086743984735)
XLA Ops:
  7.2 0.0 all-gather.3.cloned.1.call-start
  7.2 0.9 slice.48
  8.2 0.9 fusion.2
  9.1 4.0 %collective-permute-start.2 = (f32[64,640]{1,0:T(8,128)S(1)}, f32[64,640]{1,0:T(8,128)S(1)}, u32[]{:S(2)}, u32[]{:S(2)}) collective-permute-start(f32[64,640]{1,0:T(8,128)S(1)} %fusion.2), channel_id=1, source_target_pairs={{0,64},{16,80},{1,65},{17,81},{2,66},{18,82},{3,67},{19,83},{4,68}... | collective-permute-start | bytes 491528 | tf_op jit(solution)/shard_map/ppermute | solution.py:324
  13.1 2.2 %collective-permute-start.1 = (f32[64,640]{1,0:T(8,128)S(1)}, f32[64,640]{1,0:T(8,128)S(1)}, u32[]{:S(2)}, u32[]{:S(2)}) collective-permute-start(f32[64,640]{1,0:T(8,128)S(1)} %fusion.2), channel_id=1, source_target_pairs={{0,128},{16,144},{1,129},{17,145},{2,130},{18,146},{3,131},{19,147... | collective-permute-start | bytes 491528 | tf_op jit(solution)/shard_map/ppermute | solution.py:324
  15.3 1.3 collective-permute-start
  17.3 1.3 bitcast_select_fusion
  18.6 8.8 %collective-permute-start.6 = (bf16[512,512]{1,0:T(8,128)(2,1)S(1)}, bf16[512,512]{1,0:T(8,128)(2,1)S(1)}, u32[]{:S(2)}, u32[]{:S(2)}) collective-permute-start(bf16[512,512]{1,0:T(8,128)(2,1)S(1)} %fusion), channel_id=1, source_target_pairs={{0,8},{1,9},{16,24},{17,25},{32,40},{33,41},{48,56},{49,57},{64,72... | collective-permute-start | bytes 1572872 | tf_op jit(solution)/shard_map/ppermute | solution.py:336
  27.4 0.0 collective-permute-done.2
  27.5 0.0 collective-permute-done.1
  27.5 0.0 collective-permute-done
  27.5 3.2 %collective-permute-start.5 = (f32[64,640]{1,0:T(8,128)S(1)}, f32[64,640]{1,0:T(8,128)S(1)}, u32[]{:S(2)}, u32[]{:S(2)}) collective-permute-start(f32[64,640]{1,0:T(8,128)S(1)} %select_select_fusion.2), channel_id=1, source_target_pairs={{0,16},{16,32},{64,80},{80,96},{128,144},{144,160},{192,208},{208,... | collective-permute-start | bytes 491528 | tf_op jit(solution)/shard_map/ppermute | solution.py:329
  30.7 1.3 collective-permute-start.4
  32.0 1.9 %collective-permute-start.3 = (f32[64,640]{1,0:T(8,128)S(1)}, f32[64,640]{1,0:T(8,128)S(1)}, u32[]{:S(2)}, u32[]{:S(2)}) collective-permute-start(f32[64,640]{1,0:T(8,128)S(1)} %select_select_fusion.2), channel_id=1, source_target_pairs={{0,48},{16,0},{64,112},{80,64},{128,176},{144,128},{192,240},{208,... | collective-permute-start | bytes 491528 | tf_op jit(solution)/shard_map/ppermute | solution.py:329
  34.0 0.0 collective-permute-done.5
  34.0 2.4 %collective-permute-done.4 = f32[64,640]{1,0:T(8,128)S(1)} collective-permute-done((f32[64,640]{1,0:T(8,128)S(1)}, f32[64,640]{1,0:T(8,128)S(1)}, u32[]{:S(2)}, u32[]{:S(2)}) %collective-permute-start.4) | collective-permute-done | bytes 163872 | tf_op jit(solution)/shard_map/ppermute | solution.py:329
  36.5 2.3 %collective-permute-done.3 = f32[64,640]{1,0:T(8,128)S(1)} collective-permute-done((f32[64,640]{1,0:T(8,128)S(1)}, f32[64,640]{1,0:T(8,128)S(1)}, u32[]{:S(2)}, u32[]{:S(2)}) %collective-permute-start.3) | collective-permute-done | bytes 163872 | tf_op jit(solution)/shard_map/ppermute | solution.py:329
  38.8 0.7 select_select_fusion.1
  39.5 0.0 collective-permute-done.6
  39.5 0.1 fusion.1
  39.6 0.0 all-gather.3.cloned.1.call-update
  39.7 0.0 all-gather.5.cloned.1.call-start
  39.7 1.3 collective-permute-start.7
  41.1 3.8 %collective-permute-done.7 = bf16[256,512]{1,0:T(8,128)(2,1)S(1)} collective-permute-done((bf16[256,512]{1,0:T(8,128)(2,1)S(1)}, bf16[256,512]{1,0:T(8,128)(2,1)S(1)}, u32[]{:S(2)}, u32[]{:S(2)}) %collective-permute-start.7) | collective-permute-done | bytes 262176 | tf_op jit(solution)/shard_map/ppermute | solution.py:336
  45.0 1.3 collective-permute-start.9
  46.3 1.3 collective-permute-start.8
  47.6 4.8 %collective-permute-start.10 = (bf16[64,512]{1,0:T(8,128)(2,1)S(1)}, bf16[64,512]{1,0:T(8,128)(2,1)S(1)}, u32[]{:S(2)}, u32[]{:S(2)}) collective-permute-start(bf16[64,512]{1,0:T(8,128)(2,1)S(1)} %get-tuple-element.40), channel_id=1, source_target_pairs={{0,1},{1,0},{4,5},{5,4},{8,9},{9,8},{12,13},{13,12},{16,17},{17,16... | collective-permute-start | bytes 196616 | tf_op jit(solution)/shard_map/ppermute | solution.py:348
  52.4 0.0 collective-permute-done.9
  52.4 0.0 collective-permute-done.8
  52.5 0.8 collective-permute-done.10
  53.3 0.7 collective-permute-start.13
  54.0 0.7 collective-permute-start.12
  54.7 0.7 collective-permute-start.11
  55.4 0.0 collective-permute-done.12
  55.4 0.0 collective-permute-done.11
  55.4 0.7 collective-permute-start.16
  56.1 0.7 collective-permute-start.15
  56.8 1.3 collective-permute-start.14
  58.1 0.0 collective-permute-done.16
  58.1 0.0 collective-permute-done.15
  58.1 7.3 %collective-permute-done.14 = bf16[64,512]{1,0:T(8,128)(2,1)S(1)} collective-permute-done((bf16[64,512]{1,0:T(8,128)(2,1)S(1)}, bf16[64,512]{1,0:T(8,128)(2,1)S(1)}, u32[]{:S(2)}, u32[]{:S(2)}) %collective-permute-start.14) | collective-permute-done | bytes 65568 | tf_op jit(solution)/shard_map/ppermute | solution.py:329
  65.5 0.0 copy-start
  65.5 0.7 copy-done
  66.2 0.0 all-gather.5.cloned.1.call-update
  66.3 1.9 %collective-permute-start.17 = (bf16[64,512]{1,0:T(8,128)(2,1)S(1)}, bf16[64,512]{1,0:T(8,128)(2,1)S(1)}, u32[]{:S(2)}, u32[]{:S(2)}) collective-permute-start(bf16[64,512]{1,0:T(8,128)(2,1)S(1)} %pad_maximum_fusion.1), channel_id=1, source_target_pairs={{0,0},{1,16},{2,32},{3,48},{4,64},{5,80},{6,96},{7,112},{8,128},{9... | collective-permute-start | bytes 196616 | tf_op jit(solution)/shard_map/ppermute | solution.py:378
  68.2 0.7 pad_add_fusion.place
  68.9 13.8 %all-gather.3.cloned.1.call-done.raw_h = f32[1024,640]{1,0:T(8,128)} async-done(((f32[64,640]{1,0:T(8,128)}), f32[1024,640]{1,0:T(8,128)}) %all-gather.3.cloned.1.call-update) | async-done | bytes 2621456 | tf_op jit(solution)/shard_map/all_gather | solution.py:372
  82.7 28.1 %factor_first.1 = (f32[64,1024]{1,0:T(8,128)}, bf16[1024,1024]{1,0:T(8,128)(2,1)}, bf16[1024,128]{1,0:T(8,128)(2,1)}, bf16[1024,128]{1,0:T(8,128)(2,1)}) custom-call(s32[3]{0:T(128)} %pad_add_fusion.place, f32[1024,640]{1,0:T(8,128)} %all-gather.3.cloned.1.call-done.raw_h), custom_call_target="tpu_custom_call" | custom-call | tf_op jit(solution)/shard_map/factor_first/pallas_call | solution.py:384
  110.8 0.1 collective-permute-start.20
  110.9 0.1 collective-permute-start.19
  111.0 1.4 collective-permute-start.18
  112.4 5.4 %collective-permute-done.18 = bf16[64,512]{1,0:T(8,128)(2,1)S(1)} collective-permute-done((bf16[64,512]{1,0:T(8,128)(2,1)S(1)}, bf16[64,512]{1,0:T(8,128)(2,1)S(1)}, u32[]{:S(2)}, u32[]{:S(2)}) %collective-permute-start.18) | collective-permute-done | bytes 65568 | tf_op jit(solution)/shard_map/ppermute | solution.py:401
  117.8 0.0 collective-permute-done.19
  117.8 1.5 collective-permute-start.23
  119.4 0.3 collective-permute-start.22
  119.7 0.5 collective-permute-start.21
  120.2 5.9 %all-gather.5.cloned.1.call-done.tile_h.refs_4_ = bf16[1024,2816]{1,0:T(8,128)(2,1)} async-done(((bf16[64,2816]{1,0:T(8,128)(2,1)}), bf16[1024,2816]{1,0:T(8,128)(2,1)}) %all-gather.5.cloned.1.call-update) | async-done | bytes 5767184 | tf_op jit(solution)/shard_map/all_gather | solution.py:377
  126.1 35.2 %factor_second.1 = (f32[64,1024]{1,0:T(8,128)}, bf16[1024,1024]{1,0:T(8,128)(2,1)}, bf16[1024,128]{1,0:T(8,128)(2,1)}, bf16[1024,128]{1,0:T(8,128)(2,1)}, bf16[1024,512]{1,0:T(8,128)(2,1)}) custom-call(s32[3]{0:T(128)} %pad_add_fusion.place, bf16[1024,2816]{1,0:T(8,128)(2,1)} %all-gather.5.cloned.1.call-done.tile_h.refs_4_, ...), custom_call_target="tpu_custom_call" | custom-call | tf_op jit(solution)/shard_map/factor_second/pallas_call | solution.py:410
  161.3 0.0 collective-permute-done.23.refs_3_
  161.3 0.0 collective-permute-done.21.refs_1_
  161.3 0.7 copy-done.2
  162.0 0.1 copy-done.3
  162.2 0.0 copy-done.4
  162.2 16.2 %finish.1 = (f32[64,1024]{1,0:T(8,128)}, bf16[1024,768]{1,0:T(8,128)(2,1)}) custom-call(s32[3]{0:T(128)} %pad_add_fusion.place, bf16[256,512]{1,0:T(8,128)(2,1)} %copy-done.1, bf16[256,512]{1,0:T(8,128)(2,1)} %copy-done.4, bf16[256,512]{1,0:T(8,128)(2,1)} %copy-done.3, bf16[256,512]{1,0:T(8,128)(2,1)} %copy-done.2, ...), custom_call_target="tpu_custom_call" | custom-call | tf_op jit(solution)/shard_map/finish/pallas_call | solution.py:428
  (29 shorter events, 0.4 us)
Async XLA Ops:
  7.2 75.6 %all-gather.3.cloned.1.call-start = ((), (), s32[]{:S(2)}) async-start(), calls=%async_computation | async-start | bytes 2785280 | tf_op jit(solution)/shard_map/all_gather | solution.py:372
  9.1 18.3 %collective-permute-start.2 = (f32[64,640]{1,0:T(8,128)S(1)}, f32[64,640]{1,0:T(8,128)S(1)}, u32[]{:S(2)}, u32[]{:S(2)}) collective-permute-start(f32[64,640]{1,0:T(8,128)S(1)} %fusion.2), channel_id=1, source_target_pairs={{0,64},{16,80},{1,65},{17,81},{2,66},{18,82},{3,67},{19,83},{4,68}... | collective-permute-start | bytes 491528 | tf_op jit(solution)/shard_map/ppermute | solution.py:324
  13.1 14.4 %collective-permute-start.1 = (f32[64,640]{1,0:T(8,128)S(1)}, f32[64,640]{1,0:T(8,128)S(1)}, u32[]{:S(2)}, u32[]{:S(2)}) collective-permute-start(f32[64,640]{1,0:T(8,128)S(1)} %fusion.2), channel_id=1, source_target_pairs={{0,128},{16,144},{1,129},{17,145},{2,130},{18,146},{3,131},{19,147... | collective-permute-start | bytes 491528 | tf_op jit(solution)/shard_map/ppermute | solution.py:324
  15.3 12.2 %collective-permute-start = (f32[64,640]{1,0:T(8,128)S(1)}, f32[64,640]{1,0:T(8,128)S(1)}, u32[]{:S(2)}, u32[]{:S(2)}) collective-permute-start(f32[64,640]{1,0:T(8,128)S(1)} %fusion.2), channel_id=1, source_target_pairs={{0,192},{16,208},{1,193},{17,209},{2,194},{18,210},{3,195},{19,211... | collective-permute-start | bytes 491528 | tf_op jit(solution)/shard_map/ppermute | solution.py:324
  18.6 20.9 %collective-permute-start.6 = (bf16[512,512]{1,0:T(8,128)(2,1)S(1)}, bf16[512,512]{1,0:T(8,128)(2,1)S(1)}, u32[]{:S(2)}, u32[]{:S(2)}) collective-permute-start(bf16[512,512]{1,0:T(8,128)(2,1)S(1)} %fusion), channel_id=1, source_target_pairs={{0,8},{1,9},{16,24},{17,25},{32,40},{33,41},{48,56},{49,57},{64,72... | collective-permute-start | bytes 1572872 | tf_op jit(solution)/shard_map/ppermute | solution.py:336
  27.5 6.5 %collective-permute-start.5 = (f32[64,640]{1,0:T(8,128)S(1)}, f32[64,640]{1,0:T(8,128)S(1)}, u32[]{:S(2)}, u32[]{:S(2)}) collective-permute-start(f32[64,640]{1,0:T(8,128)S(1)} %select_select_fusion.2), channel_id=1, source_target_pairs={{0,16},{16,32},{64,80},{80,96},{128,144},{144,160},{192,208},{208,... | collective-permute-start | bytes 491528 | tf_op jit(solution)/shard_map/ppermute | solution.py:329
  30.7 5.7 %collective-permute-start.4 = (f32[64,640]{1,0:T(8,128)S(1)}, f32[64,640]{1,0:T(8,128)S(1)}, u32[]{:S(2)}, u32[]{:S(2)}) collective-permute-start(f32[64,640]{1,0:T(8,128)S(1)} %select_select_fusion.2), channel_id=1, source_target_pairs={{0,32},{16,48},{64,96},{80,112},{128,160},{144,176},{192,224},{208... | collective-permute-start | bytes 491528 | tf_op jit(solution)/shard_map/ppermute | solution.py:329
  32.0 6.8 %collective-permute-start.3 = (f32[64,640]{1,0:T(8,128)S(1)}, f32[64,640]{1,0:T(8,128)S(1)}, u32[]{:S(2)}, u32[]{:S(2)}) collective-permute-start(f32[64,640]{1,0:T(8,128)S(1)} %select_select_fusion.2), channel_id=1, source_target_pairs={{0,48},{16,0},{64,112},{80,64},{128,176},{144,128},{192,240},{208,... | collective-permute-start | bytes 491528 | tf_op jit(solution)/shard_map/ppermute | solution.py:329
  39.7 86.4 %all-gather.5.cloned.1.call-start = ((), (), s32[]{:S(2)}) async-start(), calls=%async_computation.1 | async-start | bytes 6127616 | tf_op jit(solution)/shard_map/all_gather | solution.py:377
  39.7 5.2 %collective-permute-start.7 = (bf16[256,512]{1,0:T(8,128)(2,1)S(1)}, bf16[256,512]{1,0:T(8,128)(2,1)S(1)}, u32[]{:S(2)}, u32[]{:S(2)}) collective-permute-start(bf16[256,512]{1,0:T(8,128)(2,1)S(1)} %slice.40), channel_id=1, source_target_pairs={{0,4},{1,5},{8,12},{9,13},{16,20},{17,21},{24,28},{25,29},{32,36},... | collective-permute-start | bytes 786440 | tf_op jit(solution)/shard_map/ppermute | solution.py:336
  45.0 7.4 %collective-permute-start.9 = (bf16[64,512]{1,0:T(8,128)(2,1)S(1)}, bf16[64,512]{1,0:T(8,128)(2,1)S(1)}, u32[]{:S(2)}, u32[]{:S(2)}) collective-permute-start(bf16[64,512]{1,0:T(8,128)(2,1)S(1)} %get-tuple-element.39), channel_id=1, source_target_pairs={{0,3},{1,2},{4,7},{5,6},{8,11},{9,10},{12,15},{13,14},{16,19},{17,... | collective-permute-start | bytes 196616 | tf_op jit(solution)/shard_map/ppermute | solution.py:348
  46.3 6.2 %collective-permute-start.8 = (bf16[64,512]{1,0:T(8,128)(2,1)S(1)}, bf16[64,512]{1,0:T(8,128)(2,1)S(1)}, u32[]{:S(2)}, u32[]{:S(2)}) collective-permute-start(bf16[64,512]{1,0:T(8,128)(2,1)S(1)} %get-tuple-element.38), channel_id=1, source_target_pairs={{0,2},{1,3},{4,6},{5,7},{8,10},{9,11},{12,14},{13,15},{16,18},{17,... | collective-permute-start | bytes 196616 | tf_op jit(solution)/shard_map/ppermute | solution.py:348
  47.6 5.7 %collective-permute-start.10 = (bf16[64,512]{1,0:T(8,128)(2,1)S(1)}, bf16[64,512]{1,0:T(8,128)(2,1)S(1)}, u32[]{:S(2)}, u32[]{:S(2)}) collective-permute-start(bf16[64,512]{1,0:T(8,128)(2,1)S(1)} %get-tuple-element.40), channel_id=1, source_target_pairs={{0,1},{1,0},{4,5},{5,4},{8,9},{9,8},{12,13},{13,12},{16,17},{17,16... | collective-permute-start | bytes 196616 | tf_op jit(solution)/shard_map/ppermute | solution.py:348
  53.3 2.1 %collective-permute-start.13 = (bf16[64,512]{1,0:T(8,128)(2,1)S(1)}, bf16[64,512]{1,0:T(8,128)(2,1)S(1)}, u32[]{:S(2)}, u32[]{:S(2)}) collective-permute-start(bf16[64,512]{1,0:T(8,128)(2,1)S(1)} %broadcast_select_fusion.2), channel_id=1, source_target_pairs={{16,80},{17,81},{18,82},{19,83},{20,84},{21,85},{22,86},{23,87},{2... | collective-permute-start | bytes 196616 | tf_op jit(solution)/shard_map/ppermute | solution.py:324
  54.0 1.4 collective-permute-start.12
  54.7 0.7 collective-permute-start.11
  55.4 2.7 %collective-permute-start.16 = (bf16[64,512]{1,0:T(8,128)(2,1)S(1)}, bf16[64,512]{1,0:T(8,128)(2,1)S(1)}, u32[]{:S(2)}, u32[]{:S(2)}) collective-permute-start(bf16[64,512]{1,0:T(8,128)(2,1)S(1)} %select_select_fusion.4), channel_id=1, source_target_pairs={{16,32},{80,96},{144,160},{208,224},{17,33},{81,97},{145,161},{209... | collective-permute-start | bytes 196616 | tf_op jit(solution)/shard_map/ppermute | solution.py:329
  56.1 2.0 %collective-permute-start.15 = (bf16[64,512]{1,0:T(8,128)(2,1)S(1)}, bf16[64,512]{1,0:T(8,128)(2,1)S(1)}, u32[]{:S(2)}, u32[]{:S(2)}) collective-permute-start(bf16[64,512]{1,0:T(8,128)(2,1)S(1)} %select_select_fusion.4), channel_id=1, source_target_pairs={{16,48},{80,112},{144,176},{208,240},{17,49},{81,113},{145,177},{2... | collective-permute-start | bytes 196616 | tf_op jit(solution)/shard_map/ppermute | solution.py:329
  56.8 8.6 %collective-permute-start.14 = (bf16[64,512]{1,0:T(8,128)(2,1)S(1)}, bf16[64,512]{1,0:T(8,128)(2,1)S(1)}, u32[]{:S(2)}, u32[]{:S(2)}) collective-permute-start(bf16[64,512]{1,0:T(8,128)(2,1)S(1)} %select_select_fusion.4), channel_id=1, source_target_pairs={{16,0},{80,64},{144,128},{208,192},{17,1},{81,65},{145,129},{209,1... | collective-permute-start | bytes 196616 | tf_op jit(solution)/shard_map/ppermute | solution.py:329
  65.5 0.7 copy-start
  66.3 44.5 %collective-permute-start.17 = (bf16[64,512]{1,0:T(8,128)(2,1)S(1)}, bf16[64,512]{1,0:T(8,128)(2,1)S(1)}, u32[]{:S(2)}, u32[]{:S(2)}) collective-permute-start(bf16[64,512]{1,0:T(8,128)(2,1)S(1)} %pad_maximum_fusion.1), channel_id=1, source_target_pairs={{0,0},{1,16},{2,32},{3,48},{4,64},{5,80},{6,96},{7,112},{8,128},{9... | collective-permute-start | bytes 196616 | tf_op jit(solution)/shard_map/ppermute | solution.py:378
  110.8 7.0 %collective-permute-start.20 = (bf16[64,512]{1,0:T(8,128)(2,1)S(1)}, bf16[64,512]{1,0:T(8,128)(2,1)S(1)}, u32[]{:S(2)}, u32[]{:S(2)}) collective-permute-start(bf16[64,512]{1,0:T(8,128)(2,1)S(1)} %collective-permute-done.17), channel_id=1, source_target_pairs={{0,192},{16,208},{32,224},{48,240},{64,0},{80,16},{96,32},{112,48}... | collective-permute-start | bytes 196616 | tf_op jit(solution)/shard_map/ppermute | solution.py:401
  110.9 6.9 %collective-permute-start.19 = (bf16[64,512]{1,0:T(8,128)(2,1)S(1)}, bf16[64,512]{1,0:T(8,128)(2,1)S(1)}, u32[]{:S(2)}, u32[]{:S(2)}) collective-permute-start(bf16[64,512]{1,0:T(8,128)(2,1)S(1)} %collective-permute-done.17), channel_id=1, source_target_pairs={{0,128},{16,144},{32,160},{48,176},{64,192},{80,208},{96,224},{112... | collective-permute-start | bytes 196616 | tf_op jit(solution)/shard_map/ppermute | solution.py:401
  111.0 6.8 %collective-permute-start.18 = (bf16[64,512]{1,0:T(8,128)(2,1)S(1)}, bf16[64,512]{1,0:T(8,128)(2,1)S(1)}, u32[]{:S(2)}, u32[]{:S(2)}) collective-permute-start(bf16[64,512]{1,0:T(8,128)(2,1)S(1)} %collective-permute-done.17), channel_id=1, source_target_pairs={{0,64},{16,80},{32,96},{48,112},{64,128},{80,144},{96,160},{112,17... | collective-permute-start | bytes 196616 | tf_op jit(solution)/shard_map/ppermute | solution.py:401
  117.8 43.5 %copy-start.1 = (bf16[256,512]{1,0:T(8,128)(2,1)}, bf16[256,512]{1,0:T(8,128)(2,1)S(1)}, u32[]{:S(2)}) copy-start(bf16[256,512]{1,0:T(8,128)(2,1)S(1)} %constant_dynamic-update-slice_fusion.refs_0_) | copy-start | bytes 786436
  117.8 43.5 %collective-permute-start.23 = (bf16[256,512]{1,0:T(8,128)(2,1)S(1)}, bf16[256,512]{1,0:T(8,128)(2,1)S(1)}, u32[]{:S(2)}, u32[]{:S(2)}) collective-permute-start(bf16[256,512]{1,0:T(8,128)(2,1)S(1)} %constant_dynamic-update-slice_fusion.refs_0_), channel_id=1, source_target_pairs={{0,48},{16,0},{32,16},{48,32},{64,112},{80,64},{96,80},{112,96},{1... | collective-permute-start | bytes 786440 | tf_op jit(solution)/shard_map/ppermute | solution.py:407
  119.4 42.0 %collective-permute-start.22 = (bf16[256,512]{1,0:T(8,128)(2,1)S(1)}, bf16[256,512]{1,0:T(8,128)(2,1)S(1)}, u32[]{:S(2)}, u32[]{:S(2)}) collective-permute-start(bf16[256,512]{1,0:T(8,128)(2,1)S(1)} %constant_dynamic-update-slice_fusion.refs_0_), channel_id=1, source_target_pairs={{0,32},{16,48},{32,0},{48,16},{64,96},{80,112},{96,64},{112,80},{1... | collective-permute-start | bytes 786440 | tf_op jit(solution)/shard_map/ppermute | solution.py:407
  119.7 41.7 %collective-permute-start.21 = (bf16[256,512]{1,0:T(8,128)(2,1)S(1)}, bf16[256,512]{1,0:T(8,128)(2,1)S(1)}, u32[]{:S(2)}, u32[]{:S(2)}) collective-permute-start(bf16[256,512]{1,0:T(8,128)(2,1)S(1)} %constant_dynamic-update-slice_fusion.refs_0_), channel_id=1, source_target_pairs={{0,16},{16,32},{32,48},{48,0},{64,80},{80,96},{96,112},{112,64},{1... | collective-permute-start | bytes 786440 | tf_op jit(solution)/shard_map/ppermute | solution.py:407
  161.3 0.7 copy-start.2
  161.3 0.8 copy-start.3
  161.3 0.8 copy-start.4
Sparse Core Ops, SparseCore 0:
  39.8 42.8 all-gather.2
  85.1 40.9 all-gather.4

commit v2 on v1

--- a/solution.py
+++ b/solution.py
@@ -15,6 +15,7 @@
 NBLK = NB // BLK
 BAND = 5 * BLK
 SPAN = 4
+BELOW = range(1, 16)
 TILE1 = 2 * BAND + 2 * RANK
 TN = (((0,), (0,)), ((), ()))
 NT = (((1,), (1,)), ((), ()))
@@ -332,8 +333,8 @@
 
 def halve(x, z, gap):
     half = x.shape[0] // 2
-    pairs = [(2 * a + c, 2 * (a + gap) + c) for a in range(0, 8, 2 * gap) for c in (0, 1)]
-    got = lax.ppermute(x[half:], "col", pairs)
+    pairs = [(at(r, 2 * a + c), at(r, 2 * (a + gap) + c)) for r in BELOW for a in range(0, 8, 2 * gap) for c in (0, 1)]
+    got = lax.ppermute(x[half:], ("row", "col"), pairs)
     return jnp.where((z // gap) % 2 == 1, got, x[:half])
 
 
@@ -344,8 +345,10 @@
         return jnp.where(first, cur[64 * q0 : 64 * q0 + 64], cur[64 * q1 : 64 * q1 + 64])
 
     def send(x, step, flip):
-        pairs = [(2 * a + c, 2 * (a + step) + (c ^ flip)) for a in range(0, 8, 2) for c in (0, 1)]
-        return lax.ppermute(after(x, *tokens), "col", pairs)
+        pairs = [
+            (at(r, 2 * a + c), at(r, 2 * (a + step) + (c ^ flip))) for r in BELOW for a in range(0, 8, 2) for c in (0, 1)
+        ]
+        return lax.ppermute(after(x, *tokens) if tokens else x, ("row", "col"), pairs)
 
     odd = z % 2 == 1
     same = jnp.where(odd, send(chunk(2, 3), 1, 0), chunk(0, 1))
@@ -367,12 +370,16 @@
 
     band = lax.dynamic_slice(jnp.concatenate([mine, mine[:, :BAND]], axis=1), (0, BLK * z), (64, BAND))
     half = halve(both, z, 4)
-    band0, band1 = spread_y(spread_x(band, row_at, (0, 1)), row_at, (0, 1))
+    (band0,) = spread_y(spread_x(band, row_at, (0,)), row_at, (0,))
     band0, half = lax.optimization_barrier((band0, half))
     raw0 = lax.all_gather(band0, "col", tiled=True)
 
-    part0, part1 = deal(halve(half, z, 2), z, core, ())
-    (first,) = spread_y(spread_x(part0, row_at, (1,)), row_at, (1,))
+    quarter = halve(half, z, 2)
+    part0, part1 = deal(quarter, z, core, ())
+    way1, part0, part1 = lax.optimization_barrier((spread_x(after(band, quarter), row_at, (1,)), part0, part1))
+    (band1,) = spread_y(way1, row_at, (1,))
+    first, band1 = lax.optimization_barrier((spread_x(part0, row_at, (1,)), band1))
+    (first,) = spread_y(first, row_at, (1,))
     hi, lo = split(band1)
     tile = lax.all_gather(jnp.concatenate([hi, lo, first, part0, part1], axis=1), "col", tiled=True)
     flip = lax.ppermute(

time: 186 us -> 193 us (1.038); the launches traced: 185 us -> 190 us
  starting transfers between devices: 42 us -> 45.5 us
    ppermute x6 -> x9, waiting for transfers between devices: 12 us -> 38.6 us  [spread_y(): lax.ppermute(x, 'row', [(4 * a + y, 4 * a + (y + s) % 4) for a in range(4...]
    ppermute x5, starting transfers between devices: 17.5 us -> 3.37 us  [the longest x3 1.99 us: send(): lax.ppermute(after(x, *tokens) if tokens else x, ('row', 'col'), pairs)]
    all_gather x1, waiting for transfers between devices: 13.8 us -> 0.01 us  [shards(): raw0 = lax.all_gather(band0, 'col', tiled=True)]
    ppermute x3, starting transfers between devices: 1.53 us -> 10 us  [shards(): lax.ppermute(flip, 'row', [(4 * a + b, 4 * ((a + s) % 4) + b) for a in ra...]
    ppermute x6 -> x9, starting transfers between devices: 9.05 us -> 15.5 us  [spread_y(): lax.ppermute(x, 'row', [(4 * a + y, 4 * a + (y + s) % 4) for a in range(4...]
    all_gather x1, waiting for transfers between devices: 5.88 us -> 0.01 us  [shards(): lax.all_gather(jnp.concatenate([hi, lo, first, part0, part1], axis=1), 'c...]
    ppermute x5, waiting for transfers between devices: 4.68 us -> 0.01 us  [the longest x3 0.01 us: send(): lax.ppermute(after(x, *tokens) if tokens else x, ('row', 'col'), pairs)]
    ppermute x6 -> x9, starting transfers between devices: 9.45 us -> 11.5 us  [spread_x(): lax.ppermute(x, 'row', [(y, 4 * k + y) for y in rows])]
  transfers between devices with their start and end apart: 26 -> 32, of which waited for: 8 -> 5; matrix products, arithmetic and copies ran while one was open for 2% -> 2% of each run, Pallas kernels for 34% -> 33%
where the time goes in v2:
time: 193 us; the launch traced here: 190 us
  Pallas kernels  79.5 us (41%)
  starting transfers between devices  45.5 us (24%)
  waiting for transfers between devices  43.1 us (22%)
  between operations  15.5 us (8%)
  other arithmetic  3.96 us (2%)
  local copies, waits for them, and re-layouts  2.56 us (1%)
    ppermute x9, waiting for transfers between devices, spread_y(): lax.ppermute(x, 'row', [(4 * a + y, 4 * a + (y + s) % 4) for a in range(4...  38.6 us
    pallas_call x1, Pallas kernels, shards(): pl.pallas_call(second_kernel, out_shape=FACTOR + [shape(NB, 2 * RANK, BF1...  35.2 us
    pallas_call x1, Pallas kernels, shards(): pl.pallas_call(first_kernel, out_shape=FACTOR, in_specs=[SMEM, ANY], out_...  28.1 us
    pallas_call x1, Pallas kernels, shards(): pl.pallas_call(last_kernel, out_shape=[shape(64, NB, F32), shape(NB, 3 *...  16.2 us
    ppermute x9, starting transfers between devices, spread_y(): lax.ppermute(x, 'row', [(4 * a + y, 4 * a + (y + s) % 4) for a in range(4...  15.5 us
    ppermute x9, starting transfers between devices, spread_x(): lax.ppermute(x, 'row', [(y, 4 * k + y) for y in rows])  11.5 us
    ppermute x3, starting transfers between devices, shards(): lax.ppermute(flip, 'row', [(4 * a + b, 4 * ((a + s) % 4) + b) for a in ra...  10 us
    ppermute x3, waiting for transfers between devices, shards(): lax.ppermute(flip, 'row', [(4 * a + b, 4 * ((a + s) % 4) + b) for a in ra...  4.35 us
  transfers between devices with their start and end apart: 32, of which 5 were waited for; matrix products, arithmetic and copies ran while one was open for 2% of the time, Pallas kernels for 33%

profile of v2, /device:TPU:1, one launch (start us, length us, event | category | flops | bytes accessed | tf_op | source)
XLA Modules:
  0.0 190.1 jit_solution(14397581784501525466)
XLA Ops:
  7.2 0.0 all-gather.3.cloned.1.call-start
  7.2 0.9 slice.48
  8.2 0.9 fusion.2
  9.1 4.0 %collective-permute-start.2 = (f32[64,640]{1,0:T(8,128)S(1)}, f32[64,640]{1,0:T(8,128)S(1)}, u32[]{:S(2)}, u32[]{:S(2)}) collective-permute-start(f32[64,640]{1,0:T(8,128)S(1)} %fusion.2), channel_id=1, source_target_pairs={{0,64},{1,65},{2,66},{3,67},{4,68},{5,69},{6,70},{7,71},{8,72},{9,... | collective-permute-start | bytes 491528 | tf_op jit(solution)/shard_map/ppermute | solution.py:325
  13.1 2.2 %collective-permute-start.1 = (f32[64,640]{1,0:T(8,128)S(1)}, f32[64,640]{1,0:T(8,128)S(1)}, u32[]{:S(2)}, u32[]{:S(2)}) collective-permute-start(f32[64,640]{1,0:T(8,128)S(1)} %fusion.2), channel_id=1, source_target_pairs={{0,128},{1,129},{2,130},{3,131},{4,132},{5,133},{6,134},{7,135},{8... | collective-permute-start | bytes 491528 | tf_op jit(solution)/shard_map/ppermute | solution.py:325
  15.3 1.3 collective-permute-start
  17.3 1.3 bitcast_select_fusion
  18.6 0.7 collective-permute-start.6
  19.3 0.0 collective-permute-done.2
  19.3 0.1 collective-permute-done.1
  19.4 0.0 collective-permute-done
  19.5 6.6 %collective-permute-start.5 = (f32[64,640]{1,0:T(8,128)S(1)}, f32[64,640]{1,0:T(8,128)S(1)}, u32[]{:S(2)}, u32[]{:S(2)}) collective-permute-start(f32[64,640]{1,0:T(8,128)S(1)} %select_select_fusion.3), channel_id=1, source_target_pairs={{0,16},{64,80},{128,144},{192,208},{1,17},{65,81},{129,145},{193,2... | collective-permute-start | bytes 491528 | tf_op jit(solution)/shard_map/ppermute | solution.py:330
  26.1 2.3 %collective-permute-start.4 = (f32[64,640]{1,0:T(8,128)S(1)}, f32[64,640]{1,0:T(8,128)S(1)}, u32[]{:S(2)}, u32[]{:S(2)}) collective-permute-start(f32[64,640]{1,0:T(8,128)S(1)} %select_select_fusion.3), channel_id=1, source_target_pairs={{0,32},{64,96},{128,160},{192,224},{1,33},{65,97},{129,161},{193,2... | collective-permute-start | bytes 491528 | tf_op jit(solution)/shard_map/ppermute | solution.py:330
  28.4 1.3 collective-permute-start.3
  29.8 2.6 %collective-permute-done.4 = f32[64,640]{1,0:T(8,128)S(1)} collective-permute-done((f32[64,640]{1,0:T(8,128)S(1)}, f32[64,640]{1,0:T(8,128)S(1)}, u32[]{:S(2)}, u32[]{:S(2)}) %collective-permute-start.4) | collective-permute-done | bytes 163872 | tf_op jit(solution)/shard_map/ppermute | solution.py:330
  32.4 0.0 collective-permute-done.3
  32.4 0.7 select_select_fusion.2
  33.1 0.0 collective-permute-done.6
  33.1 0.1 fusion.1
  33.2 0.0 all-gather.3.cloned.1.call-update
  33.2 0.0 all-gather.5.cloned.1.call-start
  33.3 0.7 collective-permute-start.7
  34.1 0.7 collective-permute-start.11
  34.8 0.7 collective-permute-start.12
  35.5 0.7 collective-permute-start.13
  36.2 0.7 collective-permute-start.10
  36.8 0.7 collective-permute-start.9
  37.5 0.7 collective-permute-start.8
  38.2 0.0 collective-permute-done.12
  38.3 0.0 collective-permute-done.10
  38.3 0.7 collective-permute-start.16
  39.0 0.7 collective-permute-start.15
  39.7 0.7 collective-permute-start.14
  40.4 0.7 collective-permute-start.19
  41.0 0.7 collective-permute-start.18
  41.7 1.3 collective-permute-start.17
  43.0 0.0 collective-permute-done.15
  43.0 0.0 collective-permute-done.14
  43.1 0.0 collective-permute-done.18
  43.1 31.9 %collective-permute-done.17 = f32[64,640]{1,0:T(8,128)S(1)} collective-permute-done((f32[64,640]{1,0:T(8,128)S(1)}, f32[64,640]{1,0:T(8,128)S(1)}, u32[]{:S(2)}, u32[]{:S(2)}) %collective-permute-start.17) | collective-permute-done | bytes 163872 | tf_op jit(solution)/shard_map/ppermute | solution.py:330
  75.1 0.7 collective-permute-start.22
  75.8 0.7 collective-permute-start.21
  76.4 1.3 collective-permute-start.20
  77.8 0.0 collective-permute-done.22
  77.8 4.0 %collective-permute-done.20 = bf16[64,512]{1,0:T(8,128)(2,1)S(1)} collective-permute-done((bf16[64,512]{1,0:T(8,128)(2,1)S(1)}, bf16[64,512]{1,0:T(8,128)(2,1)S(1)}, u32[]{:S(2)}, u32[]{:S(2)}) %collective-permute-start.20) | collective-permute-done | bytes 65568 | tf_op jit(solution)/shard_map/ppermute | solution.py:330
  81.9 0.0 copy-start
  81.9 0.7 copy-done
  82.6 0.0 all-gather.5.cloned.1.call-update
  82.7 3.4 %collective-permute-start.23 = (bf16[64,512]{1,0:T(8,128)(2,1)S(1)}, bf16[64,512]{1,0:T(8,128)(2,1)S(1)}, u32[]{:S(2)}, u32[]{:S(2)}) collective-permute-start(bf16[64,512]{1,0:T(8,128)(2,1)S(1)} %pad_maximum_fusion.1), channel_id=1, source_target_pairs={{0,0},{1,16},{2,32},{3,48},{4,64},{5,80},{6,96},{7,112},{8,128},{9... | collective-permute-start | bytes 196616 | tf_op jit(solution)/shard_map/ppermute | solution.py:385
  86.1 0.6 pad_add_fusion.place
  86.7 28.1 %factor_first.1 = (f32[64,1024]{1,0:T(8,128)}, bf16[1024,1024]{1,0:T(8,128)(2,1)}, bf16[1024,128]{1,0:T(8,128)(2,1)}, bf16[1024,128]{1,0:T(8,128)(2,1)}) custom-call(s32[3]{0:T(128)} %pad_add_fusion.place, f32[1024,640]{1,0:T(8,128)} %all-gather.3.cloned.1.call-done.raw_h), custom_call_target="tpu_custom_call" | custom-call | tf_op jit(solution)/shard_map/factor_first/pallas_call | solution.py:391
  114.8 0.0 collective-permute-done.23
  114.8 9.3 %collective-permute-start.26 = (bf16[64,512]{1,0:T(8,128)(2,1)S(1)}, bf16[64,512]{1,0:T(8,128)(2,1)S(1)}, u32[]{:S(2)}, u32[]{:S(2)}) collective-permute-start(bf16[64,512]{1,0:T(8,128)(2,1)S(1)} %collective-permute-done.23), channel_id=1, source_target_pairs={{0,192},{16,208},{32,224},{48,240},{64,0},{80,16},{96,32},{112,48}... | collective-permute-start | bytes 196616 | tf_op jit(solution)/shard_map/ppermute | solution.py:408
  124.1 0.0 collective-permute-start.25
  124.1 0.7 collective-permute-start.24
  124.8 4.3 %collective-permute-done.24 = bf16[64,512]{1,0:T(8,128)(2,1)S(1)} collective-permute-done((bf16[64,512]{1,0:T(8,128)(2,1)S(1)}, bf16[64,512]{1,0:T(8,128)(2,1)S(1)}, u32[]{:S(2)}, u32[]{:S(2)}) %collective-permute-start.24) | collective-permute-done | bytes 65568 | tf_op jit(solution)/shard_map/ppermute | solution.py:408
  129.2 0.3 collective-permute-start.29
  129.5 0.1 collective-permute-start.28
  129.6 1.4 collective-permute-start.27
  130.9 35.2 %factor_second.1 = (f32[64,1024]{1,0:T(8,128)}, bf16[1024,1024]{1,0:T(8,128)(2,1)}, bf16[1024,128]{1,0:T(8,128)(2,1)}, bf16[1024,128]{1,0:T(8,128)(2,1)}, bf16[1024,512]{1,0:T(8,128)(2,1)}) custom-call(s32[3]{0:T(128)} %pad_add_fusion.place, bf16[1024,2816]{1,0:T(8,128)(2,1)} %all-gather.5.cloned.1.call-done.tile_h.refs_4_, ...), custom_call_target="tpu_custom_call" | custom-call | tf_op jit(solution)/shard_map/factor_second/pallas_call | solution.py:417
  166.2 0.7 copy-done.2
  166.9 0.1 copy-done.3
  167.0 0.0 copy-done.4
  167.0 16.2 %finish.1 = (f32[64,1024]{1,0:T(8,128)}, bf16[1024,768]{1,0:T(8,128)(2,1)}) custom-call(s32[3]{0:T(128)} %pad_add_fusion.place, bf16[256,512]{1,0:T(8,128)(2,1)} %copy-done.1, bf16[256,512]{1,0:T(8,128)(2,1)} %copy-done.4, bf16[256,512]{1,0:T(8,128)(2,1)} %copy-done.3, bf16[256,512]{1,0:T(8,128)(2,1)} %copy-done.2, ...), custom_call_target="tpu_custom_call" | custom-call | tf_op jit(solution)/shard_map/finish/pallas_call | solution.py:435
  (43 shorter events, 0.4 us)
Async XLA Ops:
  7.2 79.5 %all-gather.3.cloned.1.call-start = ((), (), s32[]{:S(2)}) async-start(), calls=%async_computation | async-start | bytes 2785280 | tf_op jit(solution)/shard_map/all_gather | solution.py:375
  9.1 10.2 %collective-permute-start.2 = (f32[64,640]{1,0:T(8,128)S(1)}, f32[64,640]{1,0:T(8,128)S(1)}, u32[]{:S(2)}, u32[]{:S(2)}) collective-permute-start(f32[64,640]{1,0:T(8,128)S(1)} %fusion.2), channel_id=1, source_target_pairs={{0,64},{1,65},{2,66},{3,67},{4,68},{5,69},{6,70},{7,71},{8,72},{9,... | collective-permute-start | bytes 491528 | tf_op jit(solution)/shard_map/ppermute | solution.py:325
  13.1 6.4 %collective-permute-start.1 = (f32[64,640]{1,0:T(8,128)S(1)}, f32[64,640]{1,0:T(8,128)S(1)}, u32[]{:S(2)}, u32[]{:S(2)}) collective-permute-start(f32[64,640]{1,0:T(8,128)S(1)} %fusion.2), channel_id=1, source_target_pairs={{0,128},{1,129},{2,130},{3,131},{4,132},{5,133},{6,134},{7,135},{8... | collective-permute-start | bytes 491528 | tf_op jit(solution)/shard_map/ppermute | solution.py:325
  15.3 4.1 %collective-permute-start = (f32[64,640]{1,0:T(8,128)S(1)}, f32[64,640]{1,0:T(8,128)S(1)}, u32[]{:S(2)}, u32[]{:S(2)}) collective-permute-start(f32[64,640]{1,0:T(8,128)S(1)} %fusion.2), channel_id=1, source_target_pairs={{0,192},{1,193},{2,194},{3,195},{4,196},{5,197},{6,198},{7,199},{8... | collective-permute-start | bytes 491528 | tf_op jit(solution)/shard_map/ppermute | solution.py:325
  18.6 14.5 %collective-permute-start.6 = (bf16[512,512]{1,0:T(8,128)(2,1)S(1)}, bf16[512,512]{1,0:T(8,128)(2,1)S(1)}, u32[]{:S(2)}, u32[]{:S(2)}) collective-permute-start(bf16[512,512]{1,0:T(8,128)(2,1)S(1)} %fusion), channel_id=1, source_target_pairs={{16,24},{17,25},{32,40},{33,41},{48,56},{49,57},{64,72},{65,73},{8... | collective-permute-start | bytes 1572872 | tf_op jit(solution)/shard_map/ppermute | solution.py:337
  19.5 10.3 %collective-permute-start.5 = (f32[64,640]{1,0:T(8,128)S(1)}, f32[64,640]{1,0:T(8,128)S(1)}, u32[]{:S(2)}, u32[]{:S(2)}) collective-permute-start(f32[64,640]{1,0:T(8,128)S(1)} %select_select_fusion.3), channel_id=1, source_target_pairs={{0,16},{64,80},{128,144},{192,208},{1,17},{65,81},{129,145},{193,2... | collective-permute-start | bytes 491528 | tf_op jit(solution)/shard_map/ppermute | solution.py:330
  26.1 6.3 %collective-permute-start.4 = (f32[64,640]{1,0:T(8,128)S(1)}, f32[64,640]{1,0:T(8,128)S(1)}, u32[]{:S(2)}, u32[]{:S(2)}) collective-permute-start(f32[64,640]{1,0:T(8,128)S(1)} %select_select_fusion.3), channel_id=1, source_target_pairs={{0,32},{64,96},{128,160},{192,224},{1,33},{65,97},{129,161},{193,2... | collective-permute-start | bytes 491528 | tf_op jit(solution)/shard_map/ppermute | solution.py:330
  28.4 4.0 %collective-permute-start.3 = (f32[64,640]{1,0:T(8,128)S(1)}, f32[64,640]{1,0:T(8,128)S(1)}, u32[]{:S(2)}, u32[]{:S(2)}) collective-permute-start(f32[64,640]{1,0:T(8,128)S(1)} %select_select_fusion.3), channel_id=1, source_target_pairs={{0,48},{64,112},{128,176},{192,240},{1,49},{65,113},{129,177},{193... | collective-permute-start | bytes 491528 | tf_op jit(solution)/shard_map/ppermute | solution.py:330
  33.2 97.7 %all-gather.5.cloned.1.call-start = ((), (), s32[]{:S(2)}) async-start(), calls=%async_computation.1 | async-start | bytes 6127616 | tf_op jit(solution)/shard_map/all_gather | solution.py:384
  33.3 0.7 collective-permute-start.7
  34.1 3.4 %collective-permute-start.11 = (bf16[64,512]{1,0:T(8,128)(2,1)S(1)}, bf16[64,512]{1,0:T(8,128)(2,1)S(1)}, u32[]{:S(2)}, u32[]{:S(2)}) collective-permute-start(bf16[64,512]{1,0:T(8,128)(2,1)S(1)} %get-tuple-element.48), channel_id=1, source_target_pairs={{16,18},{17,19},{20,22},{21,23},{24,26},{25,27},{28,30},{29,31},{3... | collective-permute-start | bytes 196616 | tf_op jit(solution)/shard_map/ppermute | solution.py:351
  34.8 3.4 %collective-permute-start.12 = (bf16[64,512]{1,0:T(8,128)(2,1)S(1)}, bf16[64,512]{1,0:T(8,128)(2,1)S(1)}, u32[]{:S(2)}, u32[]{:S(2)}) collective-permute-start(bf16[64,512]{1,0:T(8,128)(2,1)S(1)} %get-tuple-element.49), channel_id=1, source_target_pairs={{16,19},{17,18},{20,23},{21,22},{24,27},{25,26},{28,31},{29,30},{3... | collective-permute-start | bytes 196616 | tf_op jit(solution)/shard_map/ppermute | solution.py:351
  35.5 2.7 %collective-permute-start.13 = (bf16[64,512]{1,0:T(8,128)(2,1)S(1)}, bf16[64,512]{1,0:T(8,128)(2,1)S(1)}, u32[]{:S(2)}, u32[]{:S(2)}) collective-permute-start(bf16[64,512]{1,0:T(8,128)(2,1)S(1)} %get-tuple-element.50), channel_id=1, source_target_pairs={{16,17},{17,16},{20,21},{21,20},{24,25},{25,24},{28,29},{29,28},{3... | collective-permute-start | bytes 196616 | tf_op jit(solution)/shard_map/ppermute | solution.py:351
  36.2 2.1 %collective-permute-start.10 = (f32[64,640]{1,0:T(8,128)S(1)}, f32[64,640]{1,0:T(8,128)S(1)}, u32[]{:S(2)}, u32[]{:S(2)}) collective-permute-start(f32[64,640]{1,0:T(8,128)S(1)} %fusion.2), channel_id=1, source_target_pairs={{16,80},{17,81},{18,82},{19,83},{20,84},{21,85},{22,86},{23,87},{2... | collective-permute-start | bytes 491528 | tf_op jit(solution)/shard_map/ppermute | solution.py:325
  36.8 1.4 collective-permute-start.9
  37.5 0.8 collective-permute-start.8
  38.3 3.4 %collective-permute-start.16 = (bf16[64,512]{1,0:T(8,128)(2,1)S(1)}, bf16[64,512]{1,0:T(8,128)(2,1)S(1)}, u32[]{:S(2)}, u32[]{:S(2)}) collective-permute-start(bf16[64,512]{1,0:T(8,128)(2,1)S(1)} %get-tuple-element.25), channel_id=1, source_target_pairs={{16,80},{17,81},{18,82},{19,83},{20,84},{21,85},{22,86},{23,87},{2... | collective-permute-start | bytes 196616 | tf_op jit(solution)/shard_map/ppermute | solution.py:325
  39.0 4.0 %collective-permute-start.15 = (bf16[64,512]{1,0:T(8,128)(2,1)S(1)}, bf16[64,512]{1,0:T(8,128)(2,1)S(1)}, u32[]{:S(2)}, u32[]{:S(2)}) collective-permute-start(bf16[64,512]{1,0:T(8,128)(2,1)S(1)} %get-tuple-element.25), channel_id=1, source_target_pairs={{16,144},{17,145},{18,146},{19,147},{20,148},{21,149},{22,150},{23... | collective-permute-start | bytes 196616 | tf_op jit(solution)/shard_map/ppermute | solution.py:325
  39.7 3.4 %collective-permute-start.14 = (bf16[64,512]{1,0:T(8,128)(2,1)S(1)}, bf16[64,512]{1,0:T(8,128)(2,1)S(1)}, u32[]{:S(2)}, u32[]{:S(2)}) collective-permute-start(bf16[64,512]{1,0:T(8,128)(2,1)S(1)} %get-tuple-element.25), channel_id=1, source_target_pairs={{16,208},{17,209},{18,210},{19,211},{20,212},{21,213},{22,214},{23... | collective-permute-start | bytes 196616 | tf_op jit(solution)/shard_map/ppermute | solution.py:325
  40.4 2.7 %collective-permute-start.19 = (f32[64,640]{1,0:T(8,128)S(1)}, f32[64,640]{1,0:T(8,128)S(1)}, u32[]{:S(2)}, u32[]{:S(2)}) collective-permute-start(f32[64,640]{1,0:T(8,128)S(1)} %select_select_fusion.1), channel_id=1, source_target_pairs={{16,32},{80,96},{144,160},{208,224},{17,33},{81,97},{145,161},{209... | collective-permute-start | bytes 491528 | tf_op jit(solution)/shard_map/ppermute | solution.py:330
  41.0 2.0 %collective-permute-start.18 = (f32[64,640]{1,0:T(8,128)S(1)}, f32[64,640]{1,0:T(8,128)S(1)}, u32[]{:S(2)}, u32[]{:S(2)}) collective-permute-start(f32[64,640]{1,0:T(8,128)S(1)} %select_select_fusion.1), channel_id=1, source_target_pairs={{16,48},{80,112},{144,176},{208,240},{17,49},{81,113},{145,177},{2... | collective-permute-start | bytes 491528 | tf_op jit(solution)/shard_map/ppermute | solution.py:330
  41.7 33.3 %collective-permute-start.17 = (f32[64,640]{1,0:T(8,128)S(1)}, f32[64,640]{1,0:T(8,128)S(1)}, u32[]{:S(2)}, u32[]{:S(2)}) collective-permute-start(f32[64,640]{1,0:T(8,128)S(1)} %select_select_fusion.1), channel_id=1, source_target_pairs={{16,0},{80,64},{144,128},{208,192},{17,1},{81,65},{145,129},{209,1... | collective-permute-start | bytes 491528 | tf_op jit(solution)/shard_map/ppermute | solution.py:330
  75.1 2.7 %collective-permute-start.22 = (bf16[64,512]{1,0:T(8,128)(2,1)S(1)}, bf16[64,512]{1,0:T(8,128)(2,1)S(1)}, u32[]{:S(2)}, u32[]{:S(2)}) collective-permute-start(bf16[64,512]{1,0:T(8,128)(2,1)S(1)} %select_select_fusion.5), channel_id=1, source_target_pairs={{16,32},{80,96},{144,160},{208,224},{17,33},{81,97},{145,161},{209... | collective-permute-start | bytes 196616 | tf_op jit(solution)/shard_map/ppermute | solution.py:330
  75.8 2.0 %collective-permute-start.21 = (bf16[64,512]{1,0:T(8,128)(2,1)S(1)}, bf16[64,512]{1,0:T(8,128)(2,1)S(1)}, u32[]{:S(2)}, u32[]{:S(2)}) collective-permute-start(bf16[64,512]{1,0:T(8,128)(2,1)S(1)} %select_select_fusion.5), channel_id=1, source_target_pairs={{16,48},{80,112},{144,176},{208,240},{17,49},{81,113},{145,177},{2... | collective-permute-start | bytes 196616 | tf_op jit(solution)/shard_map/ppermute | solution.py:330
  76.4 5.4 %collective-permute-start.20 = (bf16[64,512]{1,0:T(8,128)(2,1)S(1)}, bf16[64,512]{1,0:T(8,128)(2,1)S(1)}, u32[]{:S(2)}, u32[]{:S(2)}) collective-permute-start(bf16[64,512]{1,0:T(8,128)(2,1)S(1)} %select_select_fusion.5), channel_id=1, source_target_pairs={{16,0},{80,64},{144,128},{208,192},{17,1},{81,65},{145,129},{209,1... | collective-permute-start | bytes 196616 | tf_op jit(solution)/shard_map/ppermute | solution.py:330
  81.9 0.7 copy-start
  82.7 32.1 %collective-permute-start.23 = (bf16[64,512]{1,0:T(8,128)(2,1)S(1)}, bf16[64,512]{1,0:T(8,128)(2,1)S(1)}, u32[]{:S(2)}, u32[]{:S(2)}) collective-permute-start(bf16[64,512]{1,0:T(8,128)(2,1)S(1)} %pad_maximum_fusion.1), channel_id=1, source_target_pairs={{0,0},{1,16},{2,32},{3,48},{4,64},{5,80},{6,96},{7,112},{8,128},{9... | collective-permute-start | bytes 196616 | tf_op jit(solution)/shard_map/ppermute | solution.py:385
  114.8 14.4 %collective-permute-start.26 = (bf16[64,512]{1,0:T(8,128)(2,1)S(1)}, bf16[64,512]{1,0:T(8,128)(2,1)S(1)}, u32[]{:S(2)}, u32[]{:S(2)}) collective-permute-start(bf16[64,512]{1,0:T(8,128)(2,1)S(1)} %collective-permute-done.23), channel_id=1, source_target_pairs={{0,192},{16,208},{32,224},{48,240},{64,0},{80,16},{96,32},{112,48}... | collective-permute-start | bytes 196616 | tf_op jit(solution)/shard_map/ppermute | solution.py:408
  124.1 5.0 %collective-permute-start.25 = (bf16[64,512]{1,0:T(8,128)(2,1)S(1)}, bf16[64,512]{1,0:T(8,128)(2,1)S(1)}, u32[]{:S(2)}, u32[]{:S(2)}) collective-permute-start(bf16[64,512]{1,0:T(8,128)(2,1)S(1)} %collective-permute-done.23), channel_id=1, source_target_pairs={{0,128},{16,144},{32,160},{48,176},{64,192},{80,208},{96,224},{112... | collective-permute-start | bytes 196616 | tf_op jit(solution)/shard_map/ppermute | solution.py:408
  124.1 5.0 %collective-permute-start.24 = (bf16[64,512]{1,0:T(8,128)(2,1)S(1)}, bf16[64,512]{1,0:T(8,128)(2,1)S(1)}, u32[]{:S(2)}, u32[]{:S(2)}) collective-permute-start(bf16[64,512]{1,0:T(8,128)(2,1)S(1)} %collective-permute-done.23), channel_id=1, source_target_pairs={{0,64},{16,80},{32,96},{48,112},{64,128},{80,144},{96,160},{112,17... | collective-permute-start | bytes 196616 | tf_op jit(solution)/shard_map/ppermute | solution.py:408
  129.2 36.9 %copy-start.1 = (bf16[256,512]{1,0:T(8,128)(2,1)}, bf16[256,512]{1,0:T(8,128)(2,1)S(1)}, u32[]{:S(2)}) copy-start(bf16[256,512]{1,0:T(8,128)(2,1)S(1)} %constant_dynamic-update-slice_fusion.refs_0_) | copy-start | bytes 786436
  129.2 36.9 %collective-permute-start.29 = (bf16[256,512]{1,0:T(8,128)(2,1)S(1)}, bf16[256,512]{1,0:T(8,128)(2,1)S(1)}, u32[]{:S(2)}, u32[]{:S(2)}) collective-permute-start(bf16[256,512]{1,0:T(8,128)(2,1)S(1)} %constant_dynamic-update-slice_fusion.refs_0_), channel_id=1, source_target_pairs={{0,48},{16,0},{32,16},{48,32},{64,112},{80,64},{96,80},{112,96},{1... | collective-permute-start | bytes 786440 | tf_op jit(solution)/shard_map/ppermute | solution.py:414
  129.5 36.7 %collective-permute-start.28 = (bf16[256,512]{1,0:T(8,128)(2,1)S(1)}, bf16[256,512]{1,0:T(8,128)(2,1)S(1)}, u32[]{:S(2)}, u32[]{:S(2)}) collective-permute-start(bf16[256,512]{1,0:T(8,128)(2,1)S(1)} %constant_dynamic-update-slice_fusion.refs_0_), channel_id=1, source_target_pairs={{0,32},{16,48},{32,0},{48,16},{64,96},{80,112},{96,64},{112,80},{1... | collective-permute-start | bytes 786440 | tf_op jit(solution)/shard_map/ppermute | solution.py:414
  129.6 36.6 %collective-permute-start.27 = (bf16[256,512]{1,0:T(8,128)(2,1)S(1)}, bf16[256,512]{1,0:T(8,128)(2,1)S(1)}, u32[]{:S(2)}, u32[]{:S(2)}) collective-permute-start(bf16[256,512]{1,0:T(8,128)(2,1)S(1)} %constant_dynamic-update-slice_fusion.refs_0_), channel_id=1, source_target_pairs={{0,16},{16,32},{32,48},{48,0},{64,80},{80,96},{96,112},{112,64},{1... | collective-permute-start | bytes 786440 | tf_op jit(solution)/shard_map/ppermute | solution.py:414
  166.1 0.7 copy-start.2
  166.2 0.8 copy-start.3
  166.2 0.8 copy-start.4
Sparse Core Ops, SparseCore 0:
  33.4 44.0 all-gather.2
  82.8 45.3 all-gather.4

commit v3 on v1

--- a/solution.py
+++ b/solution.py
@@ -15,6 +15,7 @@
 NBLK = NB // BLK
 BAND = 5 * BLK
 SPAN = 4
+BELOW = range(1, 16)
 TILE1 = 2 * BAND + 2 * RANK
 TN = (((0,), (0,)), ((), ()))
 NT = (((1,), (1,)), ((), ()))
@@ -192,9 +193,7 @@
     x = mm3((mh[o:e, :], ml[o:e, :]), split(w[o:e, :]))
     p[o:e, :] = x.astype(BF16)
     if e < NB:
-        xs = split(x)
-        low = lb[e:, o:e]
-        w[e:, :] = w[e:, :] - (mm(low, xs[0]) + mm(low, xs[1]))
+        w[e:, :] = w[e:, :] - mm(lb[e:, o:e], p[o:e, :])
 
 
 def second_kernel(
@@ -246,7 +245,10 @@
     j = 2 * place[0] + place[1]
     i = place[2]
     x, y = i // 4, lax.rem(i, 4)
-    pairs = [(tile_h.at[:, TILE1:], rows), (tile_h.at[:, 2 * BAND : 2 * BAND + RANK], u10)]
+    def tile_part(n):
+        return tile_h.at[:, pl.ds(TILE1 + n * RANK, RANK)], rows.at[:, pl.ds(n * RANK, RANK)]
+
+    pairs = [tile_part(3), (tile_h.at[:, 2 * BAND : 2 * BAND + RANK], u10)]
     for b in range(4):
         for a in range(4):
             k = 4 * lax.rem(x + 4 - a, 4) + lax.rem(y + 4 - b, 4)
@@ -254,7 +256,7 @@
     head = len(pairs)
     pairs += [(mh0_h, mh0), (ml0_h, ml0), (mh1_h, mh1), (ml1_h, ml1), (lb0_h, lb0), (lb1_h, lb1)]
     body = len(pairs)
-    pairs += [(p10i_h, p10i), (diag_h, diag), (lrow0_h, lrow0), (lrow1_h, lrow1)]
+    pairs += [tile_part(0), tile_part(2), (p10i_h, p10i), (diag_h, diag), (lrow0_h, lrow0), (lrow1_h, lrow1)]
     copies = fetch(pairs, sems)
     for one in copies[:head]:
         one.wait()
@@ -332,8 +334,8 @@
 
 def halve(x, z, gap):
     half = x.shape[0] // 2
-    pairs = [(2 * a + c, 2 * (a + gap) + c) for a in range(0, 8, 2 * gap) for c in (0, 1)]
-    got = lax.ppermute(x[half:], "col", pairs)
+    pairs = [(at(r, 2 * a + c), at(r, 2 * (a + gap) + c)) for r in BELOW for a in range(0, 8, 2 * gap) for c in (0, 1)]
+    got = lax.ppermute(x[half:], ("row", "col"), pairs)
     return jnp.where((z // gap) % 2 == 1, got, x[:half])
 
 
@@ -448,7 +450,7 @@
             pltpu.VMEM((NB, 3 * RANK), F32),
             pltpu.VMEM((NB, RANK), BF16),
             pltpu.VMEM((NB, 3 * RANK), BF16),
-            pltpu.SemaphoreType.DMA((28,)),
+            pltpu.SemaphoreType.DMA((30,)),
         ],
         compiler_params=grant(56),
         name="finish",

time: 186 us -> 182 us (0.978)
  Pallas kernels: 79.5 us -> 75.9 us
    ppermute x2, starting transfers between devices: 10.1 us -> 1.37 us  [halve(): got = lax.ppermute(x[half:], ('row', 'col'), pairs)]
    ppermute x6, starting transfers between devices: 9.05 us -> 17.1 us  [spread_y(): lax.ppermute(x, 'row', [(4 * a + y, 4 * a + (y + s) % 4) for a in range(4...]
    ppermute x6, waiting for transfers between devices: 12 us -> 17.4 us  [spread_y(): lax.ppermute(x, 'row', [(4 * a + y, 4 * a + (y + s) % 4) for a in range(4...]
    ppermute x2, waiting for transfers between devices: 3.83 us -> 0.01 us  [halve(): got = lax.ppermute(x[half:], ('row', 'col'), pairs)]
    pallas_call x1, Pallas kernels: 16.2 us -> 13.7 us  [shards(): pl.pallas_call(last_kernel, out_shape=[shape(64, NB, F32), shape(NB, 3 *...]
where the time goes in v3:
time: 182 us
  Pallas kernels  75.9 us (42%)
  waiting for transfers between devices  43.7 us (24%)
  starting transfers between devices  40.3 us (22%)
  between operations  15.4 us (8%)
  other arithmetic  4.01 us (2%)
  local copies, waits for them, and re-layouts  2.55 us (1%)
    pallas_call x1, Pallas kernels, shards(): pl.pallas_call(second_kernel, out_shape=FACTOR + [shape(NB, 2 * RANK, BF1...  34.2 us
    pallas_call x1, Pallas kernels, shards(): pl.pallas_call(first_kernel, out_shape=FACTOR, in_specs=[SMEM, ANY], out_...  28.1 us
    ppermute x6, waiting for transfers between devices, spread_y(): lax.ppermute(x, 'row', [(4 * a + y, 4 * a + (y + s) % 4) for a in range(4...  17.4 us
    ppermute x6, starting transfers between devices, spread_y(): lax.ppermute(x, 'row', [(4 * a + y, 4 * a + (y + s) % 4) for a in range(4...  17.1 us
    all_gather x1, waiting for transfers between devices, shards(): raw0 = lax.all_gather(band0, 'col', tiled=True)  13.8 us
    pallas_call x1, Pallas kernels, shards(): pl.pallas_call(last_kernel, out_shape=[shape(64, NB, F32), shape(NB, 3 *...  13.7 us
    ppermute x6, starting transfers between devices, spread_x(): lax.ppermute(x, 'row', [(y, 4 * k + y) for y in rows])  9.45 us
    ppermute x3, starting transfers between devices, send(): return lax.ppermute(after(x, *tokens), 'col', pairs)  6.46 us
  transfers between devices with their start and end apart: 26, of which 8 were waited for; matrix products, arithmetic and copies ran while one was open for 2% of the time, Pallas kernels for 34%

profile of v3, /device:TPU:1, one launch (start us, length us, event | category | flops | bytes accessed | tf_op | source)
XLA Modules:
  0.0 181.9 jit_solution(16180644886458494913)
XLA Ops:
  7.2 0.0 all-gather.3.cloned.1.call-start
  7.2 0.9 slice.48
  8.2 0.9 fusion.2
  9.1 4.0 %collective-permute-start.2 = (f32[64,640]{1,0:T(8,128)S(1)}, f32[64,640]{1,0:T(8,128)S(1)}, u32[]{:S(2)}, u32[]{:S(2)}) collective-permute-start(f32[64,640]{1,0:T(8,128)S(1)} %fusion.2), channel_id=1, source_target_pairs={{0,64},{16,80},{1,65},{17,81},{2,66},{18,82},{3,67},{19,83},{4,68}... | collective-permute-start | bytes 491528 | tf_op jit(solution)/shard_map/ppermute | solution.py:326
  13.1 2.2 %collective-permute-start.1 = (f32[64,640]{1,0:T(8,128)S(1)}, f32[64,640]{1,0:T(8,128)S(1)}, u32[]{:S(2)}, u32[]{:S(2)}) collective-permute-start(f32[64,640]{1,0:T(8,128)S(1)} %fusion.2), channel_id=1, source_target_pairs={{0,128},{16,144},{1,129},{17,145},{2,130},{18,146},{3,131},{19,147... | collective-permute-start | bytes 491528 | tf_op jit(solution)/shard_map/ppermute | solution.py:326
  15.3 1.3 collective-permute-start
  17.3 1.3 bitcast_select_fusion
  18.6 0.7 collective-permute-start.6
  19.3 0.0 collective-permute-done.2
  19.3 0.1 collective-permute-done.1
  19.4 0.0 collective-permute-done
  19.5 11.3 %collective-permute-start.5 = (f32[64,640]{1,0:T(8,128)S(1)}, f32[64,640]{1,0:T(8,128)S(1)}, u32[]{:S(2)}, u32[]{:S(2)}) collective-permute-start(f32[64,640]{1,0:T(8,128)S(1)} %select_select_fusion.2), channel_id=1, source_target_pairs={{0,16},{16,32},{64,80},{80,96},{128,144},{144,160},{192,208},{208,... | collective-permute-start | bytes 491528 | tf_op jit(solution)/shard_map/ppermute | solution.py:331
  30.7 1.3 collective-permute-start.4
  32.0 1.9 %collective-permute-start.3 = (f32[64,640]{1,0:T(8,128)S(1)}, f32[64,640]{1,0:T(8,128)S(1)}, u32[]{:S(2)}, u32[]{:S(2)}) collective-permute-start(f32[64,640]{1,0:T(8,128)S(1)} %select_select_fusion.2), channel_id=1, source_target_pairs={{0,48},{16,0},{64,112},{80,64},{128,176},{144,128},{192,240},{208,... | collective-permute-start | bytes 491528 | tf_op jit(solution)/shard_map/ppermute | solution.py:331
  34.0 0.0 collective-permute-done.5
  34.0 2.4 %collective-permute-done.4 = f32[64,640]{1,0:T(8,128)S(1)} collective-permute-done((f32[64,640]{1,0:T(8,128)S(1)}, f32[64,640]{1,0:T(8,128)S(1)}, u32[]{:S(2)}, u32[]{:S(2)}) %collective-permute-start.4) | collective-permute-done | bytes 163872 | tf_op jit(solution)/shard_map/ppermute | solution.py:331
  36.5 2.3 %collective-permute-done.3 = f32[64,640]{1,0:T(8,128)S(1)} collective-permute-done((f32[64,640]{1,0:T(8,128)S(1)}, f32[64,640]{1,0:T(8,128)S(1)}, u32[]{:S(2)}, u32[]{:S(2)}) %collective-permute-start.3) | collective-permute-done | bytes 163872 | tf_op jit(solution)/shard_map/ppermute | solution.py:331
  38.8 0.7 select_select_fusion.1
  39.5 0.0 collective-permute-done.6
  39.5 0.1 fusion.1
  39.6 0.0 all-gather.3.cloned.1.call-update
  39.7 0.0 all-gather.5.cloned.1.call-start
  39.7 0.7 collective-permute-start.7
  40.5 0.0 collective-permute-done.7
  40.6 1.3 collective-permute-start.9
  41.9 1.3 collective-permute-start.8
  43.2 3.9 %collective-permute-start.10 = (bf16[64,512]{1,0:T(8,128)(2,1)S(1)}, bf16[64,512]{1,0:T(8,128)(2,1)S(1)}, u32[]{:S(2)}, u32[]{:S(2)}) collective-permute-start(bf16[64,512]{1,0:T(8,128)(2,1)S(1)} %get-tuple-element.40), channel_id=1, source_target_pairs={{0,1},{1,0},{4,5},{5,4},{8,9},{9,8},{12,13},{13,12},{16,17},{17,16... | collective-permute-start | bytes 196616 | tf_op jit(solution)/shard_map/ppermute | solution.py:350
  47.1 0.0 collective-permute-done.9
  47.1 0.0 collective-permute-done.8
  47.1 0.8 collective-permute-done.10
  47.9 0.7 collective-permute-start.13
  48.6 0.7 collective-permute-start.12
  49.3 0.7 collective-permute-start.11
  50.0 0.0 collective-permute-done.13
  50.0 0.0 collective-permute-done.12
  50.0 0.0 collective-permute-done.11
  50.1 0.7 collective-permute-start.16
  50.7 0.7 collective-permute-start.15
  51.4 1.3 collective-permute-start.14
  52.7 0.0 collective-permute-done.16
  52.7 12.6 %collective-permute-done.14 = bf16[64,512]{1,0:T(8,128)(2,1)S(1)} collective-permute-done((bf16[64,512]{1,0:T(8,128)(2,1)S(1)}, bf16[64,512]{1,0:T(8,128)(2,1)S(1)}, u32[]{:S(2)}, u32[]{:S(2)}) %collective-permute-start.14) | collective-permute-done | bytes 65568 | tf_op jit(solution)/shard_map/ppermute | solution.py:331
  65.5 0.0 copy-start
  65.5 0.7 copy-done
  66.2 0.0 all-gather.5.cloned.1.call-update
  66.3 1.9 %collective-permute-start.17 = (bf16[64,512]{1,0:T(8,128)(2,1)S(1)}, bf16[64,512]{1,0:T(8,128)(2,1)S(1)}, u32[]{:S(2)}, u32[]{:S(2)}) collective-permute-start(bf16[64,512]{1,0:T(8,128)(2,1)S(1)} %pad_maximum_fusion.1), channel_id=1, source_target_pairs={{0,0},{1,16},{2,32},{3,48},{4,64},{5,80},{6,96},{7,112},{8,128},{9... | collective-permute-start | bytes 196616 | tf_op jit(solution)/shard_map/ppermute | solution.py:380
  68.2 0.7 pad_add_fusion.place
  68.9 13.8 %all-gather.3.cloned.1.call-done.raw_h = f32[1024,640]{1,0:T(8,128)} async-done(((f32[64,640]{1,0:T(8,128)}), f32[1024,640]{1,0:T(8,128)}) %all-gather.3.cloned.1.call-update) | async-done | bytes 2621456 | tf_op jit(solution)/shard_map/all_gather | solution.py:374
  82.7 28.1 %factor_first.1 = (f32[64,1024]{1,0:T(8,128)}, bf16[1024,1024]{1,0:T(8,128)(2,1)}, bf16[1024,128]{1,0:T(8,128)(2,1)}, bf16[1024,128]{1,0:T(8,128)(2,1)}) custom-call(s32[3]{0:T(128)} %pad_add_fusion.place, f32[1024,640]{1,0:T(8,128)} %all-gather.3.cloned.1.call-done.raw_h), custom_call_target="tpu_custom_call" | custom-call | tf_op jit(solution)/shard_map/factor_first/pallas_call | solution.py:386
  110.8 0.1 collective-permute-start.20
  110.9 0.1 collective-permute-start.19
  111.0 1.4 collective-permute-start.18
  112.4 5.4 %collective-permute-done.18 = bf16[64,512]{1,0:T(8,128)(2,1)S(1)} collective-permute-done((bf16[64,512]{1,0:T(8,128)(2,1)S(1)}, bf16[64,512]{1,0:T(8,128)(2,1)S(1)}, u32[]{:S(2)}, u32[]{:S(2)}) %collective-permute-start.18) | collective-permute-done | bytes 65568 | tf_op jit(solution)/shard_map/ppermute | solution.py:403
  117.8 0.0 collective-permute-done.19
  117.8 1.5 collective-permute-start.23
  119.4 0.3 collective-permute-start.22
  119.7 0.5 collective-permute-start.21
  120.2 6.1 %all-gather.5.cloned.1.call-done.tile_h.refs_4_ = bf16[1024,2816]{1,0:T(8,128)(2,1)} async-done(((bf16[64,2816]{1,0:T(8,128)(2,1)}), bf16[1024,2816]{1,0:T(8,128)(2,1)}) %all-gather.5.cloned.1.call-update) | async-done | bytes 5767184 | tf_op jit(solution)/shard_map/all_gather | solution.py:379
  126.3 34.2 %factor_second.1 = (f32[64,1024]{1,0:T(8,128)}, bf16[1024,1024]{1,0:T(8,128)(2,1)}, bf16[1024,128]{1,0:T(8,128)(2,1)}, bf16[1024,128]{1,0:T(8,128)(2,1)}, bf16[1024,512]{1,0:T(8,128)(2,1)}) custom-call(s32[3]{0:T(128)} %pad_add_fusion.place, bf16[1024,2816]{1,0:T(8,128)(2,1)} %all-gather.5.cloned.1.call-done.tile_h.refs_4_, ...), custom_call_target="tpu_custom_call" | custom-call | tf_op jit(solution)/shard_map/factor_second/pallas_call | solution.py:412
  160.5 0.0 collective-permute-done.22.refs_2_
  160.5 0.0 collective-permute-done.21.refs_1_
  160.5 0.7 copy-done.2
  161.2 0.1 copy-done.3
  161.3 0.0 copy-done.4
  161.3 13.7 %finish.1 = (f32[64,1024]{1,0:T(8,128)}, bf16[1024,768]{1,0:T(8,128)(2,1)}) custom-call(s32[3]{0:T(128)} %pad_add_fusion.place, bf16[256,512]{1,0:T(8,128)(2,1)} %copy-done.1, bf16[256,512]{1,0:T(8,128)(2,1)} %copy-done.4, bf16[256,512]{1,0:T(8,128)(2,1)} %copy-done.3, bf16[256,512]{1,0:T(8,128)(2,1)} %copy-done.2, ...), custom_call_target="tpu_custom_call" | custom-call | tf_op jit(solution)/shard_map/finish/pallas_call | solution.py:430
  (29 shorter events, 0.4 us)
Async XLA Ops:
  7.2 75.6 %all-gather.3.cloned.1.call-start = ((), (), s32[]{:S(2)}) async-start(), calls=%async_computation | async-start | bytes 2785280 | tf_op jit(solution)/shard_map/all_gather | solution.py:374
  9.1 10.2 %collective-permute-start.2 = (f32[64,640]{1,0:T(8,128)S(1)}, f32[64,640]{1,0:T(8,128)S(1)}, u32[]{:S(2)}, u32[]{:S(2)}) collective-permute-start(f32[64,640]{1,0:T(8,128)S(1)} %fusion.2), channel_id=1, source_target_pairs={{0,64},{16,80},{1,65},{17,81},{2,66},{18,82},{3,67},{19,83},{4,68}... | collective-permute-start | bytes 491528 | tf_op jit(solution)/shard_map/ppermute | solution.py:326
  13.1 6.4 %collective-permute-start.1 = (f32[64,640]{1,0:T(8,128)S(1)}, f32[64,640]{1,0:T(8,128)S(1)}, u32[]{:S(2)}, u32[]{:S(2)}) collective-permute-start(f32[64,640]{1,0:T(8,128)S(1)} %fusion.2), channel_id=1, source_target_pairs={{0,128},{16,144},{1,129},{17,145},{2,130},{18,146},{3,131},{19,147... | collective-permute-start | bytes 491528 | tf_op jit(solution)/shard_map/ppermute | solution.py:326
  15.3 4.1 %collective-permute-start = (f32[64,640]{1,0:T(8,128)S(1)}, f32[64,640]{1,0:T(8,128)S(1)}, u32[]{:S(2)}, u32[]{:S(2)}) collective-permute-start(f32[64,640]{1,0:T(8,128)S(1)} %fusion.2), channel_id=1, source_target_pairs={{0,192},{16,208},{1,193},{17,209},{2,194},{18,210},{3,195},{19,211... | collective-permute-start | bytes 491528 | tf_op jit(solution)/shard_map/ppermute | solution.py:326
  18.6 20.9 %collective-permute-start.6 = (bf16[512,512]{1,0:T(8,128)(2,1)S(1)}, bf16[512,512]{1,0:T(8,128)(2,1)S(1)}, u32[]{:S(2)}, u32[]{:S(2)}) collective-permute-start(bf16[512,512]{1,0:T(8,128)(2,1)S(1)} %fusion), channel_id=1, source_target_pairs={{16,24},{17,25},{32,40},{33,41},{48,56},{49,57},{64,72},{65,73},{8... | collective-permute-start | bytes 1572872 | tf_op jit(solution)/shard_map/ppermute | solution.py:338
  19.5 14.6 %collective-permute-start.5 = (f32[64,640]{1,0:T(8,128)S(1)}, f32[64,640]{1,0:T(8,128)S(1)}, u32[]{:S(2)}, u32[]{:S(2)}) collective-permute-start(f32[64,640]{1,0:T(8,128)S(1)} %select_select_fusion.2), channel_id=1, source_target_pairs={{0,16},{16,32},{64,80},{80,96},{128,144},{144,160},{192,208},{208,... | collective-permute-start | bytes 491528 | tf_op jit(solution)/shard_map/ppermute | solution.py:331
  30.7 5.7 %collective-permute-start.4 = (f32[64,640]{1,0:T(8,128)S(1)}, f32[64,640]{1,0:T(8,128)S(1)}, u32[]{:S(2)}, u32[]{:S(2)}) collective-permute-start(f32[64,640]{1,0:T(8,128)S(1)} %select_select_fusion.2), channel_id=1, source_target_pairs={{0,32},{16,48},{64,96},{80,112},{128,160},{144,176},{192,224},{208... | collective-permute-start | bytes 491528 | tf_op jit(solution)/shard_map/ppermute | solution.py:331
  32.0 6.8 %collective-permute-start.3 = (f32[64,640]{1,0:T(8,128)S(1)}, f32[64,640]{1,0:T(8,128)S(1)}, u32[]{:S(2)}, u32[]{:S(2)}) collective-permute-start(f32[64,640]{1,0:T(8,128)S(1)} %select_select_fusion.2), channel_id=1, source_target_pairs={{0,48},{16,0},{64,112},{80,64},{128,176},{144,128},{192,240},{208,... | collective-permute-start | bytes 491528 | tf_op jit(solution)/shard_map/ppermute | solution.py:331
  39.7 86.6 %all-gather.5.cloned.1.call-start = ((), (), s32[]{:S(2)}) async-start(), calls=%async_computation.1 | async-start | bytes 6127616 | tf_op jit(solution)/shard_map/all_gather | solution.py:379
  39.7 0.7 collective-permute-start.7
  40.6 6.5 %collective-permute-start.9 = (bf16[64,512]{1,0:T(8,128)(2,1)S(1)}, bf16[64,512]{1,0:T(8,128)(2,1)S(1)}, u32[]{:S(2)}, u32[]{:S(2)}) collective-permute-start(bf16[64,512]{1,0:T(8,128)(2,1)S(1)} %get-tuple-element.39), channel_id=1, source_target_pairs={{0,3},{1,2},{4,7},{5,6},{8,11},{9,10},{12,15},{13,14},{16,19},{17,... | collective-permute-start | bytes 196616 | tf_op jit(solution)/shard_map/ppermute | solution.py:350
  41.9 5.2 %collective-permute-start.8 = (bf16[64,512]{1,0:T(8,128)(2,1)S(1)}, bf16[64,512]{1,0:T(8,128)(2,1)S(1)}, u32[]{:S(2)}, u32[]{:S(2)}) collective-permute-start(bf16[64,512]{1,0:T(8,128)(2,1)S(1)} %get-tuple-element.38), channel_id=1, source_target_pairs={{0,2},{1,3},{4,6},{5,7},{8,10},{9,11},{12,14},{13,15},{16,18},{17,... | collective-permute-start | bytes 196616 | tf_op jit(solution)/shard_map/ppermute | solution.py:350
  43.2 4.8 %collective-permute-start.10 = (bf16[64,512]{1,0:T(8,128)(2,1)S(1)}, bf16[64,512]{1,0:T(8,128)(2,1)S(1)}, u32[]{:S(2)}, u32[]{:S(2)}) collective-permute-start(bf16[64,512]{1,0:T(8,128)(2,1)S(1)} %get-tuple-element.40), channel_id=1, source_target_pairs={{0,1},{1,0},{4,5},{5,4},{8,9},{9,8},{12,13},{13,12},{16,17},{17,16... | collective-permute-start | bytes 196616 | tf_op jit(solution)/shard_map/ppermute | solution.py:350
  47.9 2.1 %collective-permute-start.13 = (bf16[64,512]{1,0:T(8,128)(2,1)S(1)}, bf16[64,512]{1,0:T(8,128)(2,1)S(1)}, u32[]{:S(2)}, u32[]{:S(2)}) collective-permute-start(bf16[64,512]{1,0:T(8,128)(2,1)S(1)} %broadcast_select_fusion.2), channel_id=1, source_target_pairs={{16,80},{17,81},{18,82},{19,83},{20,84},{21,85},{22,86},{23,87},{2... | collective-permute-start | bytes 196616 | tf_op jit(solution)/shard_map/ppermute | solution.py:326
  48.6 1.4 collective-permute-start.12
  49.3 0.7 collective-permute-start.11
  50.1 2.7 %collective-permute-start.16 = (bf16[64,512]{1,0:T(8,128)(2,1)S(1)}, bf16[64,512]{1,0:T(8,128)(2,1)S(1)}, u32[]{:S(2)}, u32[]{:S(2)}) collective-permute-start(bf16[64,512]{1,0:T(8,128)(2,1)S(1)} %select_select_fusion.4), channel_id=1, source_target_pairs={{16,32},{80,96},{144,160},{208,224},{17,33},{81,97},{145,161},{209... | collective-permute-start | bytes 196616 | tf_op jit(solution)/shard_map/ppermute | solution.py:331
  50.7 2.0 %collective-permute-start.15 = (bf16[64,512]{1,0:T(8,128)(2,1)S(1)}, bf16[64,512]{1,0:T(8,128)(2,1)S(1)}, u32[]{:S(2)}, u32[]{:S(2)}) collective-permute-start(bf16[64,512]{1,0:T(8,128)(2,1)S(1)} %select_select_fusion.4), channel_id=1, source_target_pairs={{16,48},{80,112},{144,176},{208,240},{17,49},{81,113},{145,177},{2... | collective-permute-start | bytes 196616 | tf_op jit(solution)/shard_map/ppermute | solution.py:331
  51.4 14.0 %collective-permute-start.14 = (bf16[64,512]{1,0:T(8,128)(2,1)S(1)}, bf16[64,512]{1,0:T(8,128)(2,1)S(1)}, u32[]{:S(2)}, u32[]{:S(2)}) collective-permute-start(bf16[64,512]{1,0:T(8,128)(2,1)S(1)} %select_select_fusion.4), channel_id=1, source_target_pairs={{16,0},{80,64},{144,128},{208,192},{17,1},{81,65},{145,129},{209,1... | collective-permute-start | bytes 196616 | tf_op jit(solution)/shard_map/ppermute | solution.py:331
  65.5 0.7 copy-start
  66.3 44.5 %collective-permute-start.17 = (bf16[64,512]{1,0:T(8,128)(2,1)S(1)}, bf16[64,512]{1,0:T(8,128)(2,1)S(1)}, u32[]{:S(2)}, u32[]{:S(2)}) collective-permute-start(bf16[64,512]{1,0:T(8,128)(2,1)S(1)} %pad_maximum_fusion.1), channel_id=1, source_target_pairs={{0,0},{1,16},{2,32},{3,48},{4,64},{5,80},{6,96},{7,112},{8,128},{9... | collective-permute-start | bytes 196616 | tf_op jit(solution)/shard_map/ppermute | solution.py:380
  110.8 7.0 %collective-permute-start.20 = (bf16[64,512]{1,0:T(8,128)(2,1)S(1)}, bf16[64,512]{1,0:T(8,128)(2,1)S(1)}, u32[]{:S(2)}, u32[]{:S(2)}) collective-permute-start(bf16[64,512]{1,0:T(8,128)(2,1)S(1)} %collective-permute-done.17), channel_id=1, source_target_pairs={{0,192},{16,208},{32,224},{48,240},{64,0},{80,16},{96,32},{112,48}... | collective-permute-start | bytes 196616 | tf_op jit(solution)/shard_map/ppermute | solution.py:403
  110.9 6.9 %collective-permute-start.19 = (bf16[64,512]{1,0:T(8,128)(2,1)S(1)}, bf16[64,512]{1,0:T(8,128)(2,1)S(1)}, u32[]{:S(2)}, u32[]{:S(2)}) collective-permute-start(bf16[64,512]{1,0:T(8,128)(2,1)S(1)} %collective-permute-done.17), channel_id=1, source_target_pairs={{0,128},{16,144},{32,160},{48,176},{64,192},{80,208},{96,224},{112... | collective-permute-start | bytes 196616 | tf_op jit(solution)/shard_map/ppermute | solution.py:403
  111.0 6.8 %collective-permute-start.18 = (bf16[64,512]{1,0:T(8,128)(2,1)S(1)}, bf16[64,512]{1,0:T(8,128)(2,1)S(1)}, u32[]{:S(2)}, u32[]{:S(2)}) collective-permute-start(bf16[64,512]{1,0:T(8,128)(2,1)S(1)} %collective-permute-done.17), channel_id=1, source_target_pairs={{0,64},{16,80},{32,96},{48,112},{64,128},{80,144},{96,160},{112,17... | collective-permute-start | bytes 196616 | tf_op jit(solution)/shard_map/ppermute | solution.py:403
  117.8 42.6 %copy-start.1 = (bf16[256,512]{1,0:T(8,128)(2,1)}, bf16[256,512]{1,0:T(8,128)(2,1)S(1)}, u32[]{:S(2)}) copy-start(bf16[256,512]{1,0:T(8,128)(2,1)S(1)} %constant_dynamic-update-slice_fusion.refs_0_) | copy-start | bytes 786436
  117.8 42.6 %collective-permute-start.23 = (bf16[256,512]{1,0:T(8,128)(2,1)S(1)}, bf16[256,512]{1,0:T(8,128)(2,1)S(1)}, u32[]{:S(2)}, u32[]{:S(2)}) collective-permute-start(bf16[256,512]{1,0:T(8,128)(2,1)S(1)} %constant_dynamic-update-slice_fusion.refs_0_), channel_id=1, source_target_pairs={{0,48},{16,0},{32,16},{48,32},{64,112},{80,64},{96,80},{112,96},{1... | collective-permute-start | bytes 786440 | tf_op jit(solution)/shard_map/ppermute | solution.py:409
  119.4 41.1 %collective-permute-start.22 = (bf16[256,512]{1,0:T(8,128)(2,1)S(1)}, bf16[256,512]{1,0:T(8,128)(2,1)S(1)}, u32[]{:S(2)}, u32[]{:S(2)}) collective-permute-start(bf16[256,512]{1,0:T(8,128)(2,1)S(1)} %constant_dynamic-update-slice_fusion.refs_0_), channel_id=1, source_target_pairs={{0,32},{16,48},{32,0},{48,16},{64,96},{80,112},{96,64},{112,80},{1... | collective-permute-start | bytes 786440 | tf_op jit(solution)/shard_map/ppermute | solution.py:409
  119.7 40.8 %collective-permute-start.21 = (bf16[256,512]{1,0:T(8,128)(2,1)S(1)}, bf16[256,512]{1,0:T(8,128)(2,1)S(1)}, u32[]{:S(2)}, u32[]{:S(2)}) collective-permute-start(bf16[256,512]{1,0:T(8,128)(2,1)S(1)} %constant_dynamic-update-slice_fusion.refs_0_), channel_id=1, source_target_pairs={{0,16},{16,32},{32,48},{48,0},{64,80},{80,96},{96,112},{112,64},{1... | collective-permute-start | bytes 786440 | tf_op jit(solution)/shard_map/ppermute | solution.py:409
  160.5 0.7 copy-start.2
  160.5 0.8 copy-start.3
  160.5 0.8 copy-start.4
Sparse Core Ops, SparseCore 0:
  39.8 42.8 all-gather.2
  85.1 41.0 all-gather.4

commit v4 on v3

--- a/solution.py
+++ b/solution.py
@@ -92,7 +92,7 @@
         if (g + 1) % SPAN == 0 and near < n:
             hi, lo = split(jnp.concatenate(wide, axis=0))
             wide = []
-            both = tn32(hi, hi) + (tn32(hi, lo) + tn32(lo, hi))
+            both = tn32(jnp.concatenate([hi, hi, lo], axis=0), jnp.concatenate([hi, lo, hi], axis=0))
             done = (lane >= c0 + 8 - 8 * SPAN) & (lane < c0 + 8)
             for b in range(near, n):
                 a[b] = jnp.where(done, 0.0, a[b]) - both[8 * b : 8 * b + 8]
@@ -117,7 +117,7 @@
 
 
 def mm3(a, b):
-    return mm(a[0], b[0]) + (mm(a[0], b[1]) + mm(a[1], b[0]))
+    return mm(jnp.concatenate([a[0], a[0], a[1]], axis=1), jnp.concatenate([b[0], b[1], b[0]], axis=0))
 
 
 def unfold(work, take):

time: 182 us -> 180 us (0.989)
  Pallas kernels: 75.9 us -> 71.2 us
  waiting for transfers between devices: 43.7 us -> 46 us
    all_gather x1, waiting for transfers between devices: 6.06 us -> 8.37 us  [shards(): lax.all_gather(jnp.concatenate([hi, lo, first, part0, part1], axis=1), 'c...]
    pallas_call x1, Pallas kernels: 34.2 us -> 31.9 us  [shards(): pl.pallas_call(second_kernel, out_shape=FACTOR + [shape(NB, 2 * RANK, BF1...]
    pallas_call x1, Pallas kernels: 28.1 us -> 25.9 us  [shards(): pl.pallas_call(first_kernel, out_shape=FACTOR, in_specs=[SMEM, ANY], out_...]
  transfers between devices with their start and end apart: 26 -> 26, of which waited for: 8 -> 8; matrix products, arithmetic and copies ran while one was open for 2% -> 2% of each run, Pallas kernels for 34% -> 32%
where the time goes in v4:
time: 180 us; the launch traced here: 179 us
  Pallas kernels  71.2 us (40%)
  waiting for transfers between devices  46 us (26%)
  starting transfers between devices  40.1 us (22%)
  between operations  15.4 us (9%)
  other arithmetic  4.01 us (2%)
  local copies, waits for them, and re-layouts  2.55 us (1%)
    pallas_call x1, Pallas kernels, shards(): pl.pallas_call(second_kernel, out_shape=FACTOR + [shape(NB, 2 * RANK, BF1...  31.9 us
    pallas_call x1, Pallas kernels, shards(): pl.pallas_call(first_kernel, out_shape=FACTOR, in_specs=[SMEM, ANY], out_...  25.9 us
    ppermute x6, waiting for transfers between devices, spread_y(): lax.ppermute(x, 'row', [(4 * a + y, 4 * a + (y + s) % 4) for a in range(4...  17.4 us
    ppermute x6, starting transfers between devices, spread_y(): lax.ppermute(x, 'row', [(4 * a + y, 4 * a + (y + s) % 4) for a in range(4...  17.1 us
    all_gather x1, waiting for transfers between devices, shards(): raw0 = lax.all_gather(band0, 'col', tiled=True)  13.8 us
    pallas_call x1, Pallas kernels, shards(): pl.pallas_call(last_kernel, out_shape=[shape(64, NB, F32), shape(NB, 3 *...  13.4 us
    ppermute x6, starting transfers between devices, spread_x(): lax.ppermute(x, 'row', [(y, 4 * k + y) for y in rows])  9.45 us
    all_gather x1, waiting for transfers between devices, shards(): lax.all_gather(jnp.concatenate([hi, lo, first, part0, part1], axis=1), 'c...  8.37 us
  transfers between devices with their start and end apart: 26, of which 8 were waited for; matrix products, arithmetic and copies ran while one was open for 2% of the time, Pallas kernels for 32%

profile of v4, /device:TPU:1, one launch (start us, length us, event | category | flops | bytes accessed | tf_op | source)
XLA Modules:
  0.0 179.3 jit_solution(5282353029190485694)
XLA Ops:
  7.2 0.0 all-gather.3.cloned.1.call-start
  7.2 0.9 slice.48
  8.2 0.9 fusion.2
  9.1 4.0 %collective-permute-start.2 = (f32[64,640]{1,0:T(8,128)S(1)}, f32[64,640]{1,0:T(8,128)S(1)}, u32[]{:S(2)}, u32[]{:S(2)}) collective-permute-start(f32[64,640]{1,0:T(8,128)S(1)} %fusion.2), channel_id=1, source_target_pairs={{0,64},{16,80},{1,65},{17,81},{2,66},{18,82},{3,67},{19,83},{4,68}... | collective-permute-start | bytes 491528 | tf_op jit(solution)/shard_map/ppermute | solution.py:326
  13.1 2.2 %collective-permute-start.1 = (f32[64,640]{1,0:T(8,128)S(1)}, f32[64,640]{1,0:T(8,128)S(1)}, u32[]{:S(2)}, u32[]{:S(2)}) collective-permute-start(f32[64,640]{1,0:T(8,128)S(1)} %fusion.2), channel_id=1, source_target_pairs={{0,128},{16,144},{1,129},{17,145},{2,130},{18,146},{3,131},{19,147... | collective-permute-start | bytes 491528 | tf_op jit(solution)/shard_map/ppermute | solution.py:326
  15.3 1.3 collective-permute-start
  17.3 1.3 bitcast_select_fusion
  18.6 0.7 collective-permute-start.6
  19.3 0.0 collective-permute-done.2
  19.3 0.1 collective-permute-done.1
  19.4 0.0 collective-permute-done
  19.5 11.3 %collective-permute-start.5 = (f32[64,640]{1,0:T(8,128)S(1)}, f32[64,640]{1,0:T(8,128)S(1)}, u32[]{:S(2)}, u32[]{:S(2)}) collective-permute-start(f32[64,640]{1,0:T(8,128)S(1)} %select_select_fusion.2), channel_id=1, source_target_pairs={{0,16},{16,32},{64,80},{80,96},{128,144},{144,160},{192,208},{208,... | collective-permute-start | bytes 491528 | tf_op jit(solution)/shard_map/ppermute | solution.py:331
  30.7 1.3 collective-permute-start.4
  32.0 1.9 %collective-permute-start.3 = (f32[64,640]{1,0:T(8,128)S(1)}, f32[64,640]{1,0:T(8,128)S(1)}, u32[]{:S(2)}, u32[]{:S(2)}) collective-permute-start(f32[64,640]{1,0:T(8,128)S(1)} %select_select_fusion.2), channel_id=1, source_target_pairs={{0,48},{16,0},{64,112},{80,64},{128,176},{144,128},{192,240},{208,... | collective-permute-start | bytes 491528 | tf_op jit(solution)/shard_map/ppermute | solution.py:331
  34.0 0.0 collective-permute-done.5
  34.0 2.4 %collective-permute-done.4 = f32[64,640]{1,0:T(8,128)S(1)} collective-permute-done((f32[64,640]{1,0:T(8,128)S(1)}, f32[64,640]{1,0:T(8,128)S(1)}, u32[]{:S(2)}, u32[]{:S(2)}) %collective-permute-start.4) | collective-permute-done | bytes 163872 | tf_op jit(solution)/shard_map/ppermute | solution.py:331
  36.5 2.3 %collective-permute-done.3 = f32[64,640]{1,0:T(8,128)S(1)} collective-permute-done((f32[64,640]{1,0:T(8,128)S(1)}, f32[64,640]{1,0:T(8,128)S(1)}, u32[]{:S(2)}, u32[]{:S(2)}) %collective-permute-start.3) | collective-permute-done | bytes 163872 | tf_op jit(solution)/shard_map/ppermute | solution.py:331
  38.8 0.7 select_select_fusion.1
  39.5 0.0 collective-permute-done.6
  39.5 0.1 fusion.1
  39.6 0.0 all-gather.3.cloned.1.call-update
  39.7 0.0 all-gather.5.cloned.1.call-start
  39.7 0.7 collective-permute-start.7
  40.5 0.0 collective-permute-done.7
  40.6 1.3 collective-permute-start.9
  41.9 1.3 collective-permute-start.8
  43.2 3.9 %collective-permute-start.10 = (bf16[64,512]{1,0:T(8,128)(2,1)S(1)}, bf16[64,512]{1,0:T(8,128)(2,1)S(1)}, u32[]{:S(2)}, u32[]{:S(2)}) collective-permute-start(bf16[64,512]{1,0:T(8,128)(2,1)S(1)} %get-tuple-element.40), channel_id=1, source_target_pairs={{0,1},{1,0},{4,5},{5,4},{8,9},{9,8},{12,13},{13,12},{16,17},{17,16... | collective-permute-start | bytes 196616 | tf_op jit(solution)/shard_map/ppermute | solution.py:350
  47.1 0.0 collective-permute-done.9
  47.1 0.0 collective-permute-done.8
  47.1 0.8 collective-permute-done.10
  47.9 0.7 collective-permute-start.13
  48.6 0.7 collective-permute-start.12
  49.3 0.7 collective-permute-start.11
  50.0 0.0 collective-permute-done.13
  50.0 0.0 collective-permute-done.12
  50.0 0.0 collective-permute-done.11
  50.1 0.7 collective-permute-start.16
  50.7 0.7 collective-permute-start.15
  51.4 1.3 collective-permute-start.14
  52.7 0.0 collective-permute-done.15
  52.7 12.6 %collective-permute-done.14 = bf16[64,512]{1,0:T(8,128)(2,1)S(1)} collective-permute-done((bf16[64,512]{1,0:T(8,128)(2,1)S(1)}, bf16[64,512]{1,0:T(8,128)(2,1)S(1)}, u32[]{:S(2)}, u32[]{:S(2)}) %collective-permute-start.14) | collective-permute-done | bytes 65568 | tf_op jit(solution)/shard_map/ppermute | solution.py:331
  65.5 0.0 copy-start
  65.5 0.7 copy-done
  66.2 0.0 all-gather.5.cloned.1.call-update
  66.3 1.9 %collective-permute-start.17 = (bf16[64,512]{1,0:T(8,128)(2,1)S(1)}, bf16[64,512]{1,0:T(8,128)(2,1)S(1)}, u32[]{:S(2)}, u32[]{:S(2)}) collective-permute-start(bf16[64,512]{1,0:T(8,128)(2,1)S(1)} %pad_maximum_fusion.1), channel_id=1, source_target_pairs={{0,0},{1,16},{2,32},{3,48},{4,64},{5,80},{6,96},{7,112},{8,128},{9... | collective-permute-start | bytes 196616 | tf_op jit(solution)/shard_map/ppermute | solution.py:380
  68.2 0.7 pad_add_fusion.place
  68.9 13.8 %all-gather.3.cloned.1.call-done.raw_h = f32[1024,640]{1,0:T(8,128)} async-done(((f32[64,640]{1,0:T(8,128)}), f32[1024,640]{1,0:T(8,128)}) %all-gather.3.cloned.1.call-update) | async-done | bytes 2621456 | tf_op jit(solution)/shard_map/all_gather | solution.py:374
  82.7 25.9 %factor_first.1 = (f32[64,1024]{1,0:T(8,128)}, bf16[1024,1024]{1,0:T(8,128)(2,1)}, bf16[1024,128]{1,0:T(8,128)(2,1)}, bf16[1024,128]{1,0:T(8,128)(2,1)}) custom-call(s32[3]{0:T(128)} %pad_add_fusion.place, f32[1024,640]{1,0:T(8,128)} %all-gather.3.cloned.1.call-done.raw_h), custom_call_target="tpu_custom_call" | custom-call | tf_op jit(solution)/shard_map/factor_first/pallas_call | solution.py:386
  108.7 0.1 collective-permute-start.20
  108.8 0.1 collective-permute-start.19
  108.9 1.4 collective-permute-start.18
  110.2 5.4 %collective-permute-done.18 = bf16[64,512]{1,0:T(8,128)(2,1)S(1)} collective-permute-done((bf16[64,512]{1,0:T(8,128)(2,1)S(1)}, bf16[64,512]{1,0:T(8,128)(2,1)S(1)}, u32[]{:S(2)}, u32[]{:S(2)}) %collective-permute-start.18) | collective-permute-done | bytes 65568 | tf_op jit(solution)/shard_map/ppermute | solution.py:403
  115.6 0.0 collective-permute-done.19
  115.7 1.5 collective-permute-start.23
  117.2 0.3 collective-permute-start.22
  117.5 0.4 collective-permute-start.21
  117.9 8.4 %all-gather.5.cloned.1.call-done.tile_h.refs_4_ = bf16[1024,2816]{1,0:T(8,128)(2,1)} async-done(((bf16[64,2816]{1,0:T(8,128)(2,1)}), bf16[1024,2816]{1,0:T(8,128)(2,1)}) %all-gather.5.cloned.1.call-update) | async-done | bytes 5767184 | tf_op jit(solution)/shard_map/all_gather | solution.py:379
  126.3 31.9 %factor_second.1 = (f32[64,1024]{1,0:T(8,128)}, bf16[1024,1024]{1,0:T(8,128)(2,1)}, bf16[1024,128]{1,0:T(8,128)(2,1)}, bf16[1024,128]{1,0:T(8,128)(2,1)}, bf16[1024,512]{1,0:T(8,128)(2,1)}) custom-call(s32[3]{0:T(128)} %pad_add_fusion.place, bf16[1024,2816]{1,0:T(8,128)(2,1)} %all-gather.5.cloned.1.call-done.tile_h.refs_4_, ...), custom_call_target="tpu_custom_call" | custom-call | tf_op jit(solution)/shard_map/factor_second/pallas_call | solution.py:412
  158.2 0.0 collective-permute-done.22.refs_2_
  158.2 0.0 collective-permute-done.21.refs_1_
  158.2 0.7 copy-done.2
  158.9 0.1 copy-done.3
  159.0 0.0 copy-done.4
  159.1 13.4 %finish.1 = (f32[64,1024]{1,0:T(8,128)}, bf16[1024,768]{1,0:T(8,128)(2,1)}) custom-call(s32[3]{0:T(128)} %pad_add_fusion.place, bf16[256,512]{1,0:T(8,128)(2,1)} %copy-done.1, bf16[256,512]{1,0:T(8,128)(2,1)} %copy-done.4, bf16[256,512]{1,0:T(8,128)(2,1)} %copy-done.3, bf16[256,512]{1,0:T(8,128)(2,1)} %copy-done.2, ...), custom_call_target="tpu_custom_call" | custom-call | tf_op jit(solution)/shard_map/finish/pallas_call | solution.py:430
  (29 shorter events, 0.4 us)
Async XLA Ops:
  7.2 75.6 %all-gather.3.cloned.1.call-start = ((), (), s32[]{:S(2)}) async-start(), calls=%async_computation | async-start | bytes 2785280 | tf_op jit(solution)/shard_map/all_gather | solution.py:374
  9.1 10.2 %collective-permute-start.2 = (f32[64,640]{1,0:T(8,128)S(1)}, f32[64,640]{1,0:T(8,128)S(1)}, u32[]{:S(2)}, u32[]{:S(2)}) collective-permute-start(f32[64,640]{1,0:T(8,128)S(1)} %fusion.2), channel_id=1, source_target_pairs={{0,64},{16,80},{1,65},{17,81},{2,66},{18,82},{3,67},{19,83},{4,68}... | collective-permute-start | bytes 491528 | tf_op jit(solution)/shard_map/ppermute | solution.py:326
  13.1 6.4 %collective-permute-start.1 = (f32[64,640]{1,0:T(8,128)S(1)}, f32[64,640]{1,0:T(8,128)S(1)}, u32[]{:S(2)}, u32[]{:S(2)}) collective-permute-start(f32[64,640]{1,0:T(8,128)S(1)} %fusion.2), channel_id=1, source_target_pairs={{0,128},{16,144},{1,129},{17,145},{2,130},{18,146},{3,131},{19,147... | collective-permute-start | bytes 491528 | tf_op jit(solution)/shard_map/ppermute | solution.py:326
  15.3 4.1 %collective-permute-start = (f32[64,640]{1,0:T(8,128)S(1)}, f32[64,640]{1,0:T(8,128)S(1)}, u32[]{:S(2)}, u32[]{:S(2)}) collective-permute-start(f32[64,640]{1,0:T(8,128)S(1)} %fusion.2), channel_id=1, source_target_pairs={{0,192},{16,208},{1,193},{17,209},{2,194},{18,210},{3,195},{19,211... | collective-permute-start | bytes 491528 | tf_op jit(solution)/shard_map/ppermute | solution.py:326
  18.6 20.9 %collective-permute-start.6 = (bf16[512,512]{1,0:T(8,128)(2,1)S(1)}, bf16[512,512]{1,0:T(8,128)(2,1)S(1)}, u32[]{:S(2)}, u32[]{:S(2)}) collective-permute-start(bf16[512,512]{1,0:T(8,128)(2,1)S(1)} %fusion), channel_id=1, source_target_pairs={{16,24},{17,25},{32,40},{33,41},{48,56},{49,57},{64,72},{65,73},{8... | collective-permute-start | bytes 1572872 | tf_op jit(solution)/shard_map/ppermute | solution.py:338
  19.5 14.6 %collective-permute-start.5 = (f32[64,640]{1,0:T(8,128)S(1)}, f32[64,640]{1,0:T(8,128)S(1)}, u32[]{:S(2)}, u32[]{:S(2)}) collective-permute-start(f32[64,640]{1,0:T(8,128)S(1)} %select_select_fusion.2), channel_id=1, source_target_pairs={{0,16},{16,32},{64,80},{80,96},{128,144},{144,160},{192,208},{208,... | collective-permute-start | bytes 491528 | tf_op jit(solution)/shard_map/ppermute | solution.py:331
  30.7 5.7 %collective-permute-start.4 = (f32[64,640]{1,0:T(8,128)S(1)}, f32[64,640]{1,0:T(8,128)S(1)}, u32[]{:S(2)}, u32[]{:S(2)}) collective-permute-start(f32[64,640]{1,0:T(8,128)S(1)} %select_select_fusion.2), channel_id=1, source_target_pairs={{0,32},{16,48},{64,96},{80,112},{128,160},{144,176},{192,224},{208... | collective-permute-start | bytes 491528 | tf_op jit(solution)/shard_map/ppermute | solution.py:331
  32.0 6.8 %collective-permute-start.3 = (f32[64,640]{1,0:T(8,128)S(1)}, f32[64,640]{1,0:T(8,128)S(1)}, u32[]{:S(2)}, u32[]{:S(2)}) collective-permute-start(f32[64,640]{1,0:T(8,128)S(1)} %select_select_fusion.2), channel_id=1, source_target_pairs={{0,48},{16,0},{64,112},{80,64},{128,176},{144,128},{192,240},{208,... | collective-permute-start | bytes 491528 | tf_op jit(solution)/shard_map/ppermute | solution.py:331
  39.7 86.6 %all-gather.5.cloned.1.call-start = ((), (), s32[]{:S(2)}) async-start(), calls=%async_computation.1 | async-start | bytes 6127616 | tf_op jit(solution)/shard_map/all_gather | solution.py:379
  39.7 0.7 collective-permute-start.7
  40.6 6.5 %collective-permute-start.9 = (bf16[64,512]{1,0:T(8,128)(2,1)S(1)}, bf16[64,512]{1,0:T(8,128)(2,1)S(1)}, u32[]{:S(2)}, u32[]{:S(2)}) collective-permute-start(bf16[64,512]{1,0:T(8,128)(2,1)S(1)} %get-tuple-element.39), channel_id=1, source_target_pairs={{0,3},{1,2},{4,7},{5,6},{8,11},{9,10},{12,15},{13,14},{16,19},{17,... | collective-permute-start | bytes 196616 | tf_op jit(solution)/shard_map/ppermute | solution.py:350
  41.9 5.2 %collective-permute-start.8 = (bf16[64,512]{1,0:T(8,128)(2,1)S(1)}, bf16[64,512]{1,0:T(8,128)(2,1)S(1)}, u32[]{:S(2)}, u32[]{:S(2)}) collective-permute-start(bf16[64,512]{1,0:T(8,128)(2,1)S(1)} %get-tuple-element.38), channel_id=1, source_target_pairs={{0,2},{1,3},{4,6},{5,7},{8,10},{9,11},{12,14},{13,15},{16,18},{17,... | collective-permute-start | bytes 196616 | tf_op jit(solution)/shard_map/ppermute | solution.py:350
  43.2 4.8 %collective-permute-start.10 = (bf16[64,512]{1,0:T(8,128)(2,1)S(1)}, bf16[64,512]{1,0:T(8,128)(2,1)S(1)}, u32[]{:S(2)}, u32[]{:S(2)}) collective-permute-start(bf16[64,512]{1,0:T(8,128)(2,1)S(1)} %get-tuple-element.40), channel_id=1, source_target_pairs={{0,1},{1,0},{4,5},{5,4},{8,9},{9,8},{12,13},{13,12},{16,17},{17,16... | collective-permute-start | bytes 196616 | tf_op jit(solution)/shard_map/ppermute | solution.py:350
  47.9 2.1 %collective-permute-start.13 = (bf16[64,512]{1,0:T(8,128)(2,1)S(1)}, bf16[64,512]{1,0:T(8,128)(2,1)S(1)}, u32[]{:S(2)}, u32[]{:S(2)}) collective-permute-start(bf16[64,512]{1,0:T(8,128)(2,1)S(1)} %broadcast_select_fusion.2), channel_id=1, source_target_pairs={{16,80},{17,81},{18,82},{19,83},{20,84},{21,85},{22,86},{23,87},{2... | collective-permute-start | bytes 196616 | tf_op jit(solution)/shard_map/ppermute | solution.py:326
  48.6 1.4 collective-permute-start.12
  49.3 0.7 collective-permute-start.11
  50.1 2.7 %collective-permute-start.16 = (bf16[64,512]{1,0:T(8,128)(2,1)S(1)}, bf16[64,512]{1,0:T(8,128)(2,1)S(1)}, u32[]{:S(2)}, u32[]{:S(2)}) collective-permute-start(bf16[64,512]{1,0:T(8,128)(2,1)S(1)} %select_select_fusion.4), channel_id=1, source_target_pairs={{16,32},{80,96},{144,160},{208,224},{17,33},{81,97},{145,161},{209... | collective-permute-start | bytes 196616 | tf_op jit(solution)/shard_map/ppermute | solution.py:331
  50.7 2.0 %collective-permute-start.15 = (bf16[64,512]{1,0:T(8,128)(2,1)S(1)}, bf16[64,512]{1,0:T(8,128)(2,1)S(1)}, u32[]{:S(2)}, u32[]{:S(2)}) collective-permute-start(bf16[64,512]{1,0:T(8,128)(2,1)S(1)} %select_select_fusion.4), channel_id=1, source_target_pairs={{16,48},{80,112},{144,176},{208,240},{17,49},{81,113},{145,177},{2... | collective-permute-start | bytes 196616 | tf_op jit(solution)/shard_map/ppermute | solution.py:331
  51.4 14.0 %collective-permute-start.14 = (bf16[64,512]{1,0:T(8,128)(2,1)S(1)}, bf16[64,512]{1,0:T(8,128)(2,1)S(1)}, u32[]{:S(2)}, u32[]{:S(2)}) collective-permute-start(bf16[64,512]{1,0:T(8,128)(2,1)S(1)} %select_select_fusion.4), channel_id=1, source_target_pairs={{16,0},{80,64},{144,128},{208,192},{17,1},{81,65},{145,129},{209,1... | collective-permute-start | bytes 196616 | tf_op jit(solution)/shard_map/ppermute | solution.py:331
  65.5 0.7 copy-start
  66.3 42.4 %collective-permute-start.17 = (bf16[64,512]{1,0:T(8,128)(2,1)S(1)}, bf16[64,512]{1,0:T(8,128)(2,1)S(1)}, u32[]{:S(2)}, u32[]{:S(2)}) collective-permute-start(bf16[64,512]{1,0:T(8,128)(2,1)S(1)} %pad_maximum_fusion.1), channel_id=1, source_target_pairs={{0,0},{1,16},{2,32},{3,48},{4,64},{5,80},{6,96},{7,112},{8,128},{9... | collective-permute-start | bytes 196616 | tf_op jit(solution)/shard_map/ppermute | solution.py:380
  108.7 7.0 %collective-permute-start.20 = (bf16[64,512]{1,0:T(8,128)(2,1)S(1)}, bf16[64,512]{1,0:T(8,128)(2,1)S(1)}, u32[]{:S(2)}, u32[]{:S(2)}) collective-permute-start(bf16[64,512]{1,0:T(8,128)(2,1)S(1)} %collective-permute-done.17), channel_id=1, source_target_pairs={{0,192},{16,208},{32,224},{48,240},{64,0},{80,16},{96,32},{112,48}... | collective-permute-start | bytes 196616 | tf_op jit(solution)/shard_map/ppermute | solution.py:403
  108.8 6.9 %collective-permute-start.19 = (bf16[64,512]{1,0:T(8,128)(2,1)S(1)}, bf16[64,512]{1,0:T(8,128)(2,1)S(1)}, u32[]{:S(2)}, u32[]{:S(2)}) collective-permute-start(bf16[64,512]{1,0:T(8,128)(2,1)S(1)} %collective-permute-done.17), channel_id=1, source_target_pairs={{0,128},{16,144},{32,160},{48,176},{64,192},{80,208},{96,224},{112... | collective-permute-start | bytes 196616 | tf_op jit(solution)/shard_map/ppermute | solution.py:403
  108.9 6.8 %collective-permute-start.18 = (bf16[64,512]{1,0:T(8,128)(2,1)S(1)}, bf16[64,512]{1,0:T(8,128)(2,1)S(1)}, u32[]{:S(2)}, u32[]{:S(2)}) collective-permute-start(bf16[64,512]{1,0:T(8,128)(2,1)S(1)} %collective-permute-done.17), channel_id=1, source_target_pairs={{0,64},{16,80},{32,96},{48,112},{64,128},{80,144},{96,160},{112,17... | collective-permute-start | bytes 196616 | tf_op jit(solution)/shard_map/ppermute | solution.py:403
  115.7 42.5 %copy-start.1 = (bf16[256,512]{1,0:T(8,128)(2,1)}, bf16[256,512]{1,0:T(8,128)(2,1)S(1)}, u32[]{:S(2)}) copy-start(bf16[256,512]{1,0:T(8,128)(2,1)S(1)} %constant_dynamic-update-slice_fusion.refs_0_) | copy-start | bytes 786436
  115.7 42.5 %collective-permute-start.23 = (bf16[256,512]{1,0:T(8,128)(2,1)S(1)}, bf16[256,512]{1,0:T(8,128)(2,1)S(1)}, u32[]{:S(2)}, u32[]{:S(2)}) collective-permute-start(bf16[256,512]{1,0:T(8,128)(2,1)S(1)} %constant_dynamic-update-slice_fusion.refs_0_), channel_id=1, source_target_pairs={{0,48},{16,0},{32,16},{48,32},{64,112},{80,64},{96,80},{112,96},{1... | collective-permute-start | bytes 786440 | tf_op jit(solution)/shard_map/ppermute | solution.py:409
  117.2 41.0 %collective-permute-start.22 = (bf16[256,512]{1,0:T(8,128)(2,1)S(1)}, bf16[256,512]{1,0:T(8,128)(2,1)S(1)}, u32[]{:S(2)}, u32[]{:S(2)}) collective-permute-start(bf16[256,512]{1,0:T(8,128)(2,1)S(1)} %constant_dynamic-update-slice_fusion.refs_0_), channel_id=1, source_target_pairs={{0,32},{16,48},{32,0},{48,16},{64,96},{80,112},{96,64},{112,80},{1... | collective-permute-start | bytes 786440 | tf_op jit(solution)/shard_map/ppermute | solution.py:409
  117.5 40.7 %collective-permute-start.21 = (bf16[256,512]{1,0:T(8,128)(2,1)S(1)}, bf16[256,512]{1,0:T(8,128)(2,1)S(1)}, u32[]{:S(2)}, u32[]{:S(2)}) collective-permute-start(bf16[256,512]{1,0:T(8,128)(2,1)S(1)} %constant_dynamic-update-slice_fusion.refs_0_), channel_id=1, source_target_pairs={{0,16},{16,32},{32,48},{48,0},{64,80},{80,96},{96,112},{112,64},{1... | collective-permute-start | bytes 786440 | tf_op jit(solution)/shard_map/ppermute | solution.py:409
  158.2 0.7 copy-start.2
  158.2 0.8 copy-start.3
  158.2 0.8 copy-start.4
Sparse Core Ops, SparseCore 0:
  39.8 42.8 all-gather.2
  85.1 41.0 all-gather.4
